TPU v7x, 1024 devices: a whole 4x4x32 slice. The times are simulated.
1024 devices in a mesh: gz: 128 (over y_lo, z, core), gy: 8 (over x, y_hi).
Axes of the slice: x: 4, y: 4 (y_hi: 2, y_lo: 2; y = y_hi * 2 + y_lo), z: 32, core: 2. Of those that a mesh axis runs over, the one named last changes fastest.
Arguments:
- cell_type: int32 [2048, 3072], P('gz', 'gy'), may hold values from 0 to 3, as said below
- perturb: int32 [2048, 3072], P('gz', 'gy'), may hold values from -4 to 4
- velocity: float32 [3, 2048, 3072], P(None, 'gz', 'gy'), may hold values from -0.25 to 0.25
Outputs:
- temperature: float32 [2048, 3072], P('gz', 'gy')
- flow: float32 [3, 2048, 3072], P(None, 'gz', 'gy')
- nusselt: float32 [], replicated
Inputs may be any that keep to these rules, and one draw needn't show every extreme that they name: `cell_type`: cells with x = 0, x = 23, z = 0 or z = 2047 are adiabatic walls unless y = 0 (hot) or y = 128 - 1 (cold); inside, a few scattered wall cells of all three kinds stand among fluid cells.
All inputs are finite; a program needn't handle non-finite values.
Results may differ from a plain program's by a relative error of at most 0.0003.
Values sent between devices are 32-bit elements; how exact they have to be, the bound alone decides.
No kernel may reach another device: no remote copies, remote signals or barrier semaphores. Data moves between devices by JAX's collectives and lax.ppermute only.
A program may use at most 32 MiB of HBM per device.

v0:
```python
import jax
import jax.numpy as jnp
from jax import lax
from jax.sharding import PartitionSpec as P

NX = 24
STEPS = 8


TAU_F = 0.52
TAU_G = 0.5376
LAT19 = [
    (0, 0, 0),
    (1, 0, 0),
    (-1, 0, 0),
    (0, 1, 0),
    (0, -1, 0),
    (0, 0, 1),
    (0, 0, -1),
    (1, 1, 0),
    (-1, -1, 0),
    (1, -1, 0),
    (-1, 1, 0),
    (1, 0, 1),
    (-1, 0, -1),
    (1, 0, -1),
    (-1, 0, 1),
    (0, 1, 1),
    (0, -1, -1),
    (0, 1, -1),
    (0, -1, 1),
]
WGT19 = [1.0 / 3.0] + [1.0 / 18.0] * 6 + [1.0 / 36.0] * 12
LAT7 = LAT19[:7]
WGT7 = [0.25] + [0.125] * 6


def with_halo(cells, sides, width):
    for axis, dim in sides:
        count = lax.axis_size(axis)
        ends = count - 1
        head = lax.slice_in_dim(cells, 0, width, axis=dim)
        tail = lax.slice_in_dim(cells, cells.shape[dim] - width, cells.shape[dim], axis=dim)
        cells = jnp.concatenate(
            [
                lax.ppermute(tail, axis, [(i, (i + 1) % count) for i in range(ends)]),
                cells,
                lax.ppermute(head, axis, [((i + 1) % count, i) for i in range(ends)]),
            ],
            axis=dim,
        )
    return cells


def opposite(table, index):
    back = tuple((-v for v in table[index]))
    return table.index(back)


def build_state(cell_type, perturb, velocity, zpos, height):
    fluid = cell_type == 0
    speeds = [jnp.where(fluid, velocity[a], 0.0) for a in range(3)]
    base = 0.5 - 0.75 * (zpos + 0.5) / height + 0.05 * perturb.astype(jnp.float32)
    walls = jnp.where(cell_type == 2, 0.5, jnp.where(cell_type == 3, -0.5, 0.0))
    temp = jnp.where(fluid, base, walls)
    usq = speeds[0] ** 2 + speeds[1] ** 2 + speeds[2] ** 2
    chans = []
    for i in range(19):
        cvec = LAT19[i]
        proj = cvec[0] * speeds[0] + cvec[1] * speeds[1] + cvec[2] * speeds[2]
        chans.append(WGT19[i] * (1.0 + 3.0 * proj + 4.5 * proj * proj - 1.5 * usq))
    for j in range(7):
        cvec = LAT7[j]
        proj = cvec[0] * speeds[0] + cvec[1] * speeds[1] + cvec[2] * speeds[2]
        chans.append(WGT7[j] * temp * (1.0 + 4.0 * proj))
    chans.append((cell_type + 1).astype(jnp.float32))
    return jnp.stack(chans)


def moments(state):
    kind = state[26]
    fluid = kind == 1.0
    rho = sum((state[i] for i in range(19)))
    safe = jnp.where(fluid, rho, 1.0)
    speeds = [
        sum((LAT19[i][a] * state[i] for i in range(19) if LAT19[i][a] != 0)) / safe
        for a in range(3)
    ]
    speeds = [jnp.where(fluid, s, 0.0) for s in speeds]
    temp = sum((state[19 + j] for j in range(7)))
    return (rho, speeds, temp, fluid)


def collide_stream(state, depth_cells):
    rho, speeds, temp, fluid = moments(state)
    usq = speeds[0] ** 2 + speeds[1] ** 2 + speeds[2] ** 2
    post = []
    for i in range(19):
        cvec = LAT19[i]
        proj = cvec[0] * speeds[0] + cvec[1] * speeds[1] + cvec[2] * speeds[2]
        equil = WGT19[i] * rho * (1.0 + 3.0 * proj + 4.5 * proj * proj - 1.5 * usq)
        post.append(state[i] + (equil - state[i]) / TAU_F)
    for j in range(7):
        cvec = LAT7[j]
        proj = cvec[0] * speeds[0] + cvec[1] * speeds[1] + cvec[2] * speeds[2]
        equil = WGT7[j] * temp * (1.0 + 4.0 * proj)
        post.append(state[19 + j] + (equil - state[19 + j]) / TAU_G)
    post.append(state[26])
    post = jnp.stack(post)
    padded = jnp.pad(post, ((0, 0), (0, 0), (1, 1)))
    zcount = state.shape[1] - 2
    lcount = state.shape[2] - 2 * depth_cells

    def source(chan, cvec):
        offset = cvec[1] * depth_cells + cvec[0]
        zlow = 1 - cvec[2]
        llow = depth_cells + 1 - offset
        return padded[chan, zlow : zlow + zcount, llow : llow + lcount]

    center = post[:, 1 : 1 + zcount, depth_cells : depth_cells + lcount]
    before = state[:, 1 : 1 + zcount, depth_cells : depth_cells + lcount]
    cfluid = center[26] == 1.0
    result = []
    for i in range(19):
        skind = source(26, LAT19[i])
        moved = jnp.where(skind == 1.0, source(i, LAT19[i]), center[opposite(LAT19, i)])
        result.append(jnp.where(cfluid, moved, before[i]))
    for j in range(7):
        skind = source(26, LAT7[j])
        bounce = center[19 + opposite(LAT7, j)]
        hotside = skind == 3.0
        coldside = skind == 4.0
        wall_temp = jnp.where(hotside, 0.5, -0.5)
        anti = -bounce + 2.0 * WGT7[j] * wall_temp
        moved = jnp.where(
            skind == 1.0, source(19 + j, LAT7[j]), jnp.where(hotside | coldside, anti, bounce)
        )
        result.append(jnp.where(cfluid, moved, before[19 + j]))
    result.append(center[26])
    return jnp.stack(result)


def hot_terms(previous, final_state):
    zcount = final_state.shape[1]
    lcount = final_state.shape[2]
    below_hot = previous[26, 1 : 1 + zcount, 0:lcount] == 3.0
    rho, speeds, temp, fluid = moments(final_state)
    return (jnp.sum(jnp.where(fluid & below_hot, 0.5 - temp, 0.0)), temp, speeds)


def body(cell_type, perturb, velocity):
    slab_cells = cell_type.shape[0]
    height = slab_cells * lax.axis_size("gz")
    zpos = (lax.axis_index("gz") * slab_cells + jnp.arange(slab_cells, dtype=jnp.int32)).astype(
        jnp.float32
    )[:, None]
    state = build_state(cell_type, perturb, velocity, zpos, height)
    rim = 1
    start_prev = jnp.zeros(
        (state.shape[0], state.shape[1] + 2, state.shape[2] + 2 * NX), jnp.float32
    )

    def one_block(block_index, carried):
        current, last_input = carried
        wide = with_halo(current, (("gz", 1),), rim)
        wide = with_halo(wide, (("gy", 2),), rim * NX)
        last_input = wide
        wide = collide_stream(wide, NX)
        return (wide, last_input)

    state, previous = lax.fori_loop(0, STEPS // rim, one_block, (state, start_prev))
    total, temp, speeds = hot_terms(previous, state)
    total = lax.psum(total, ("gz", "gy"))
    nusselt = total * (2.0 / (NX * height))
    return (temp, jnp.stack(speeds), nusselt)


def solution(mesh):
    return jax.shard_map(
        body,
        mesh=mesh,
        in_specs=(P("gz", "gy"), P("gz", "gy"), P(None, "gz", "gy")),
        out_specs=(P("gz", "gy"), P(None, "gz", "gy"), P()),
        check_vma=False,
    )
```

profile of v0, /device:TPU:1, one launch (start us, length us, event | category | flops | bytes accessed | tf_op | source)
XLA Modules:
  0.0 449.1 jit_solution(12060273338897013294)
XLA Ops:
  0.7 0.8 constant_dynamic-update-slice_fusion.80
  2.1 264.3 %while.12 = (s32[]{:T(128)}, f32[27,16,384]{2,1,0:T(8,128)S(1)}, f32[27,18,432]{2,1,0:T(8,128)}, s32[]{:T(128)}) while((s32[]{:T(128)}, f32[27,16,384]{2,1,0:T(8,128)S(1)}, f32[27,18,432]{2,1,0:T(8,128)}, s32[]{:T(128)}) %tuple.152), condition=%wide.region_1.2_spmd, body=%wide.region_0.1_spmd.sunk | while | flops 5093760 | bytes 40503408 | solution.py:171
  2.2 16.1 %collective-permute-start = (f32[27,1,384]{2,1,0:T(1,128)S(1)}, f32[27,1,384]{2,1,0:T(1,128)S(1)}, u32[]{:S(2)}, u32[]{:S(2)}) collective-permute-start(f32[27,1,384]{2,1,0:T(1,128)S(1)} %get-tuple-element.229), channel_id=1, source_target_pairs={{8,0},{16,8},{24,16},{32,24},{40,32},{48,40},{56,48},{64,56},{72,6... | collective-permute-start | bytes 124424 | tf_op jit(solution)/shard_map/while/body/eval_jaxpr/ppermute | solution.py:48
  18.3 1.9 collective-permute-start.1
  20.2 1.2 collective-permute-done.1
  21.6 1.3 collective-permute-start.2
  22.9 5.5 %collective-permute-start.3 = (f32[27,18,24]{2,1,0:T(8,128)S(1)}, f32[27,18,24]{2,1,0:T(8,128)S(1)}, u32[]{:S(2)}, u32[]{:S(2)}) collective-permute-start(f32[27,18,24]{2,1,0:T(8,128)S(1)} %get-tuple-element.232), channel_id=1, source_target_pairs={{0,1},{1,2},{2,3},{3,4},{4,5},{5,6},{6,7},{8,9},{9,10},{10,11},{11... | collective-permute-start | bytes 139976 | tf_op jit(solution)/shard_map/while/body/eval_jaxpr/ppermute | solution.py:46
  28.4 6.3 %collective-permute-done.2 = f32[27,18,24]{2,1,0:T(8,128)S(1)} collective-permute-done((f32[27,18,24]{2,1,0:T(8,128)S(1)}, f32[27,18,24]{2,1,0:T(8,128)S(1)}, u32[]{:S(2)}, u32[]{:S(2)}) %collective-permute-start.2) | collective-permute-done | bytes 46688 | tf_op jit(solution)/shard_map/while/body/eval_jaxpr/ppermute | solution.py:48
  35.1 0.8 pad_maximum_fusion.26
  39.8 3.2 collective-permute-start
  43.0 2.4 collective-permute-start.1
  45.3 1.1 collective-permute-done.1
  46.6 1.3 collective-permute-start.2
  47.9 6.3 %collective-permute-start.3 = (f32[27,18,24]{2,1,0:T(8,128)S(1)}, f32[27,18,24]{2,1,0:T(8,128)S(1)}, u32[]{:S(2)}, u32[]{:S(2)}) collective-permute-start(f32[27,18,24]{2,1,0:T(8,128)S(1)} %get-tuple-element.232), channel_id=1, source_target_pairs={{0,1},{1,2},{2,3},{3,4},{4,5},{5,6},{6,7},{8,9},{9,10},{10,11},{11... | collective-permute-start | bytes 139976 | tf_op jit(solution)/shard_map/while/body/eval_jaxpr/ppermute | solution.py:46
  54.2 6.4 %collective-permute-done.2 = f32[27,18,24]{2,1,0:T(8,128)S(1)} collective-permute-done((f32[27,18,24]{2,1,0:T(8,128)S(1)}, f32[27,18,24]{2,1,0:T(8,128)S(1)}, u32[]{:S(2)}, u32[]{:S(2)}) %collective-permute-start.2) | collective-permute-done | bytes 46688 | tf_op jit(solution)/shard_map/while/body/eval_jaxpr/ppermute | solution.py:48
  60.6 7.7 %collective-permute-done.3 = f32[27,18,24]{2,1,0:T(8,128)S(1)} collective-permute-done((f32[27,18,24]{2,1,0:T(8,128)S(1)}, f32[27,18,24]{2,1,0:T(8,128)S(1)}, u32[]{:S(2)}, u32[]{:S(2)}) %collective-permute-start.3) | collective-permute-done | bytes 46688 | tf_op jit(solution)/shard_map/while/body/eval_jaxpr/ppermute | solution.py:46
  68.3 0.8 pad_maximum_fusion.26
  72.9 2.3 collective-permute-start
  75.2 3.2 collective-permute-start.1
  78.5 1.1 collective-permute-done.1
  79.8 1.3 collective-permute-start.2
  81.1 6.3 %collective-permute-start.3 = (f32[27,18,24]{2,1,0:T(8,128)S(1)}, f32[27,18,24]{2,1,0:T(8,128)S(1)}, u32[]{:S(2)}, u32[]{:S(2)}) collective-permute-start(f32[27,18,24]{2,1,0:T(8,128)S(1)} %get-tuple-element.232), channel_id=1, source_target_pairs={{0,1},{1,2},{2,3},{3,4},{4,5},{5,6},{6,7},{8,9},{9,10},{10,11},{11... | collective-permute-start | bytes 139976 | tf_op jit(solution)/shard_map/while/body/eval_jaxpr/ppermute | solution.py:46
  87.3 5.2 %collective-permute-done.2 = f32[27,18,24]{2,1,0:T(8,128)S(1)} collective-permute-done((f32[27,18,24]{2,1,0:T(8,128)S(1)}, f32[27,18,24]{2,1,0:T(8,128)S(1)}, u32[]{:S(2)}, u32[]{:S(2)}) %collective-permute-start.2) | collective-permute-done | bytes 46688 | tf_op jit(solution)/shard_map/while/body/eval_jaxpr/ppermute | solution.py:48
  92.6 8.3 %collective-permute-done.3 = f32[27,18,24]{2,1,0:T(8,128)S(1)} collective-permute-done((f32[27,18,24]{2,1,0:T(8,128)S(1)}, f32[27,18,24]{2,1,0:T(8,128)S(1)}, u32[]{:S(2)}, u32[]{:S(2)}) %collective-permute-start.3) | collective-permute-done | bytes 46688 | tf_op jit(solution)/shard_map/while/body/eval_jaxpr/ppermute | solution.py:46
  100.9 0.8 pad_maximum_fusion.26
  105.5 2.2 collective-permute-start
  107.7 3.4 collective-permute-start.1
  111.1 1.1 collective-permute-done.1
  112.4 1.3 collective-permute-start.2
  113.7 6.2 %collective-permute-start.3 = (f32[27,18,24]{2,1,0:T(8,128)S(1)}, f32[27,18,24]{2,1,0:T(8,128)S(1)}, u32[]{:S(2)}, u32[]{:S(2)}) collective-permute-start(f32[27,18,24]{2,1,0:T(8,128)S(1)} %get-tuple-element.232), channel_id=1, source_target_pairs={{0,1},{1,2},{2,3},{3,4},{4,5},{5,6},{6,7},{8,9},{9,10},{10,11},{11... | collective-permute-start | bytes 139976 | tf_op jit(solution)/shard_map/while/body/eval_jaxpr/ppermute | solution.py:46
  119.9 5.2 %collective-permute-done.2 = f32[27,18,24]{2,1,0:T(8,128)S(1)} collective-permute-done((f32[27,18,24]{2,1,0:T(8,128)S(1)}, f32[27,18,24]{2,1,0:T(8,128)S(1)}, u32[]{:S(2)}, u32[]{:S(2)}) %collective-permute-start.2) | collective-permute-done | bytes 46688 | tf_op jit(solution)/shard_map/while/body/eval_jaxpr/ppermute | solution.py:48
  125.1 8.3 %collective-permute-done.3 = f32[27,18,24]{2,1,0:T(8,128)S(1)} collective-permute-done((f32[27,18,24]{2,1,0:T(8,128)S(1)}, f32[27,18,24]{2,1,0:T(8,128)S(1)}, u32[]{:S(2)}, u32[]{:S(2)}) %collective-permute-start.3) | collective-permute-done | bytes 46688 | tf_op jit(solution)/shard_map/while/body/eval_jaxpr/ppermute | solution.py:46
  133.4 0.8 pad_maximum_fusion.26
  138.0 2.2 collective-permute-start
  140.2 3.4 collective-permute-start.1
  143.6 1.1 collective-permute-done.1
  144.9 1.3 collective-permute-start.2
  146.2 6.1 %collective-permute-start.3 = (f32[27,18,24]{2,1,0:T(8,128)S(1)}, f32[27,18,24]{2,1,0:T(8,128)S(1)}, u32[]{:S(2)}, u32[]{:S(2)}) collective-permute-start(f32[27,18,24]{2,1,0:T(8,128)S(1)} %get-tuple-element.232), channel_id=1, source_target_pairs={{0,1},{1,2},{2,3},{3,4},{4,5},{5,6},{6,7},{8,9},{9,10},{10,11},{11... | collective-permute-start | bytes 139976 | tf_op jit(solution)/shard_map/while/body/eval_jaxpr/ppermute | solution.py:46
  152.4 5.2 %collective-permute-done.2 = f32[27,18,24]{2,1,0:T(8,128)S(1)} collective-permute-done((f32[27,18,24]{2,1,0:T(8,128)S(1)}, f32[27,18,24]{2,1,0:T(8,128)S(1)}, u32[]{:S(2)}, u32[]{:S(2)}) %collective-permute-start.2) | collective-permute-done | bytes 46688 | tf_op jit(solution)/shard_map/while/body/eval_jaxpr/ppermute | solution.py:48
  157.6 8.3 %collective-permute-done.3 = f32[27,18,24]{2,1,0:T(8,128)S(1)} collective-permute-done((f32[27,18,24]{2,1,0:T(8,128)S(1)}, f32[27,18,24]{2,1,0:T(8,128)S(1)}, u32[]{:S(2)}, u32[]{:S(2)}) %collective-permute-start.3) | collective-permute-done | bytes 46688 | tf_op jit(solution)/shard_map/while/body/eval_jaxpr/ppermute | solution.py:46
  165.9 0.8 pad_maximum_fusion.26
  170.5 2.2 collective-permute-start
  172.7 3.4 collective-permute-start.1
  176.1 1.1 collective-permute-done.1
  177.4 1.3 collective-permute-start.2
  178.7 6.2 %collective-permute-start.3 = (f32[27,18,24]{2,1,0:T(8,128)S(1)}, f32[27,18,24]{2,1,0:T(8,128)S(1)}, u32[]{:S(2)}, u32[]{:S(2)}) collective-permute-start(f32[27,18,24]{2,1,0:T(8,128)S(1)} %get-tuple-element.232), channel_id=1, source_target_pairs={{0,1},{1,2},{2,3},{3,4},{4,5},{5,6},{6,7},{8,9},{9,10},{10,11},{11... | collective-permute-start | bytes 139976 | tf_op jit(solution)/shard_map/while/body/eval_jaxpr/ppermute | solution.py:46
  184.9 5.1 %collective-permute-done.2 = f32[27,18,24]{2,1,0:T(8,128)S(1)} collective-permute-done((f32[27,18,24]{2,1,0:T(8,128)S(1)}, f32[27,18,24]{2,1,0:T(8,128)S(1)}, u32[]{:S(2)}, u32[]{:S(2)}) %collective-permute-start.2) | collective-permute-done | bytes 46688 | tf_op jit(solution)/shard_map/while/body/eval_jaxpr/ppermute | solution.py:48
  190.1 7.9 %collective-permute-done.3 = f32[27,18,24]{2,1,0:T(8,128)S(1)} collective-permute-done((f32[27,18,24]{2,1,0:T(8,128)S(1)}, f32[27,18,24]{2,1,0:T(8,128)S(1)}, u32[]{:S(2)}, u32[]{:S(2)}) %collective-permute-start.3) | collective-permute-done | bytes 46688 | tf_op jit(solution)/shard_map/while/body/eval_jaxpr/ppermute | solution.py:46
  202.6 2.2 collective-permute-start
  204.8 5.2 %collective-permute-start.1 = (f32[27,1,384]{2,1,0:T(1,128)S(1)}, f32[27,1,384]{2,1,0:T(1,128)S(1)}, u32[]{:S(2)}, u32[]{:S(2)}) collective-permute-start(f32[27,1,384]{2,1,0:T(1,128)S(1)} %get-tuple-element.230), channel_id=1, source_target_pairs={{0,8},{8,16},{16,24},{24,32},{32,40},{40,48},{48,56},{56,64},{64,7... | collective-permute-start | bytes 124424 | tf_op jit(solution)/shard_map/while/body/eval_jaxpr/ppermute | solution.py:46
  210.0 1.1 collective-permute-done.1
  211.3 1.3 collective-permute-start.2
  212.6 6.2 %collective-permute-start.3 = (f32[27,18,24]{2,1,0:T(8,128)S(1)}, f32[27,18,24]{2,1,0:T(8,128)S(1)}, u32[]{:S(2)}, u32[]{:S(2)}) collective-permute-start(f32[27,18,24]{2,1,0:T(8,128)S(1)} %get-tuple-element.232), channel_id=1, source_target_pairs={{0,1},{1,2},{2,3},{3,4},{4,5},{5,6},{6,7},{8,9},{9,10},{10,11},{11... | collective-permute-start | bytes 139976 | tf_op jit(solution)/shard_map/while/body/eval_jaxpr/ppermute | solution.py:46
  218.8 3.3 collective-permute-done.2
  222.1 7.9 %collective-permute-done.3 = f32[27,18,24]{2,1,0:T(8,128)S(1)} collective-permute-done((f32[27,18,24]{2,1,0:T(8,128)S(1)}, f32[27,18,24]{2,1,0:T(8,128)S(1)}, u32[]{:S(2)}, u32[]{:S(2)}) %collective-permute-start.3) | collective-permute-done | bytes 46688 | tf_op jit(solution)/shard_map/while/body/eval_jaxpr/ppermute | solution.py:46
  234.7 2.1 collective-permute-start
  236.8 7.1 %collective-permute-start.1 = (f32[27,1,384]{2,1,0:T(1,128)S(1)}, f32[27,1,384]{2,1,0:T(1,128)S(1)}, u32[]{:S(2)}, u32[]{:S(2)}) collective-permute-start(f32[27,1,384]{2,1,0:T(1,128)S(1)} %get-tuple-element.230), channel_id=1, source_target_pairs={{0,8},{8,16},{16,24},{24,32},{32,40},{40,48},{48,56},{56,64},{64,7... | collective-permute-start | bytes 124424 | tf_op jit(solution)/shard_map/while/body/eval_jaxpr/ppermute | solution.py:46
  243.9 1.1 collective-permute-done.1
  245.2 1.3 collective-permute-start.2
  246.5 6.2 %collective-permute-start.3 = (f32[27,18,24]{2,1,0:T(8,128)S(1)}, f32[27,18,24]{2,1,0:T(8,128)S(1)}, u32[]{:S(2)}, u32[]{:S(2)}) collective-permute-start(f32[27,18,24]{2,1,0:T(8,128)S(1)} %get-tuple-element.232), channel_id=1, source_target_pairs={{0,1},{1,2},{2,3},{3,4},{4,5},{5,6},{6,7},{8,9},{9,10},{10,11},{11... | collective-permute-start | bytes 139976 | tf_op jit(solution)/shard_map/while/body/eval_jaxpr/ppermute | solution.py:46
  252.7 2.5 collective-permute-done.2
  255.3 6.7 %collective-permute-done.3 = f32[27,18,24]{2,1,0:T(8,128)S(1)} collective-permute-done((f32[27,18,24]{2,1,0:T(8,128)S(1)}, f32[27,18,24]{2,1,0:T(8,128)S(1)}, u32[]{:S(2)}, u32[]{:S(2)}) %collective-permute-start.3) | collective-permute-done | bytes 46688 | tf_op jit(solution)/shard_map/while/body/eval_jaxpr/ppermute | solution.py:46
  266.5 2.0 select_reduce_fusion
  269.2 178.1 %psum.7 = f32[]{:T(128)} all-reduce(f32[]{:T(128)} %get-tuple-element.105), channel_id=1, replica_groups=mesh['gz'=128,'gy'=8] {'gz','gy'}, use_global_device_ids=true, to_apply=%region_3.4 | all-reduce | flops 1 | bytes 8 | tf_op jit(solution)/shard_map/psum | solution.py:173
  (520 shorter events, 33.2 us)
Async XLA Ops:
  0.6 1.3 copy-start.1
  0.6 1.3 copy-start.2
  2.2 18.0 %collective-permute-start = (f32[27,1,384]{2,1,0:T(1,128)S(1)}, f32[27,1,384]{2,1,0:T(1,128)S(1)}, u32[]{:S(2)}, u32[]{:S(2)}) collective-permute-start(f32[27,1,384]{2,1,0:T(1,128)S(1)} %get-tuple-element.229), channel_id=1, source_target_pairs={{8,0},{16,8},{24,16},{32,24},{40,32},{48,40},{56,48},{64,56},{72,6... | collective-permute-start | bytes 124424 | tf_op jit(solution)/shard_map/while/body/eval_jaxpr/ppermute | solution.py:48
  18.3 3.1 collective-permute-start.1
  21.6 13.1 %collective-permute-start.2 = (f32[27,18,24]{2,1,0:T(8,128)S(1)}, f32[27,18,24]{2,1,0:T(8,128)S(1)}, u32[]{:S(2)}, u32[]{:S(2)}) collective-permute-start(f32[27,18,24]{2,1,0:T(8,128)S(1)} %get-tuple-element.231), channel_id=1, source_target_pairs={{1,0},{2,1},{3,2},{4,3},{5,4},{6,5},{7,6},{9,8},{10,9},{11,10},{12... | collective-permute-start | bytes 139976 | tf_op jit(solution)/shard_map/while/body/eval_jaxpr/ppermute | solution.py:48
  22.9 12.2 %collective-permute-start.3 = (f32[27,18,24]{2,1,0:T(8,128)S(1)}, f32[27,18,24]{2,1,0:T(8,128)S(1)}, u32[]{:S(2)}, u32[]{:S(2)}) collective-permute-start(f32[27,18,24]{2,1,0:T(8,128)S(1)} %get-tuple-element.232), channel_id=1, source_target_pairs={{0,1},{1,2},{2,3},{3,4},{4,5},{5,6},{6,7},{8,9},{9,10},{10,11},{11... | collective-permute-start | bytes 139976 | tf_op jit(solution)/shard_map/while/body/eval_jaxpr/ppermute | solution.py:46
  36.0 1.1 copy-start
  39.8 5.6 %collective-permute-start = (f32[27,1,384]{2,1,0:T(1,128)S(1)}, f32[27,1,384]{2,1,0:T(1,128)S(1)}, u32[]{:S(2)}, u32[]{:S(2)}) collective-permute-start(f32[27,1,384]{2,1,0:T(1,128)S(1)} %get-tuple-element.229), channel_id=1, source_target_pairs={{8,0},{16,8},{24,16},{32,24},{40,32},{48,40},{56,48},{64,56},{72,6... | collective-permute-start | bytes 124424 | tf_op jit(solution)/shard_map/while/body/eval_jaxpr/ppermute | solution.py:48
  43.0 3.5 collective-permute-start.1
  46.6 13.9 %collective-permute-start.2 = (f32[27,18,24]{2,1,0:T(8,128)S(1)}, f32[27,18,24]{2,1,0:T(8,128)S(1)}, u32[]{:S(2)}, u32[]{:S(2)}) collective-permute-start(f32[27,18,24]{2,1,0:T(8,128)S(1)} %get-tuple-element.231), channel_id=1, source_target_pairs={{1,0},{2,1},{3,2},{4,3},{5,4},{6,5},{7,6},{9,8},{10,9},{11,10},{12... | collective-permute-start | bytes 139976 | tf_op jit(solution)/shard_map/while/body/eval_jaxpr/ppermute | solution.py:48
  47.9 20.3 %collective-permute-start.3 = (f32[27,18,24]{2,1,0:T(8,128)S(1)}, f32[27,18,24]{2,1,0:T(8,128)S(1)}, u32[]{:S(2)}, u32[]{:S(2)}) collective-permute-start(f32[27,18,24]{2,1,0:T(8,128)S(1)} %get-tuple-element.232), channel_id=1, source_target_pairs={{0,1},{1,2},{2,3},{3,4},{4,5},{5,6},{6,7},{8,9},{9,10},{10,11},{11... | collective-permute-start | bytes 139976 | tf_op jit(solution)/shard_map/while/body/eval_jaxpr/ppermute | solution.py:46
  69.1 1.1 copy-start
  72.9 5.6 %collective-permute-start = (f32[27,1,384]{2,1,0:T(1,128)S(1)}, f32[27,1,384]{2,1,0:T(1,128)S(1)}, u32[]{:S(2)}, u32[]{:S(2)}) collective-permute-start(f32[27,1,384]{2,1,0:T(1,128)S(1)} %get-tuple-element.229), channel_id=1, source_target_pairs={{8,0},{16,8},{24,16},{32,24},{40,32},{48,40},{56,48},{64,56},{72,6... | collective-permute-start | bytes 124424 | tf_op jit(solution)/shard_map/while/body/eval_jaxpr/ppermute | solution.py:48
  75.2 4.3 collective-permute-start.1
  79.8 12.8 %collective-permute-start.2 = (f32[27,18,24]{2,1,0:T(8,128)S(1)}, f32[27,18,24]{2,1,0:T(8,128)S(1)}, u32[]{:S(2)}, u32[]{:S(2)}) collective-permute-start(f32[27,18,24]{2,1,0:T(8,128)S(1)} %get-tuple-element.231), channel_id=1, source_target_pairs={{1,0},{2,1},{3,2},{4,3},{5,4},{6,5},{7,6},{9,8},{10,9},{11,10},{12... | collective-permute-start | bytes 139976 | tf_op jit(solution)/shard_map/while/body/eval_jaxpr/ppermute | solution.py:48
  81.1 19.8 %collective-permute-start.3 = (f32[27,18,24]{2,1,0:T(8,128)S(1)}, f32[27,18,24]{2,1,0:T(8,128)S(1)}, u32[]{:S(2)}, u32[]{:S(2)}) collective-permute-start(f32[27,18,24]{2,1,0:T(8,128)S(1)} %get-tuple-element.232), channel_id=1, source_target_pairs={{0,1},{1,2},{2,3},{3,4},{4,5},{5,6},{6,7},{8,9},{9,10},{10,11},{11... | collective-permute-start | bytes 139976 | tf_op jit(solution)/shard_map/while/body/eval_jaxpr/ppermute | solution.py:46
  101.7 1.1 copy-start
  105.5 5.6 %collective-permute-start = (f32[27,1,384]{2,1,0:T(1,128)S(1)}, f32[27,1,384]{2,1,0:T(1,128)S(1)}, u32[]{:S(2)}, u32[]{:S(2)}) collective-permute-start(f32[27,1,384]{2,1,0:T(1,128)S(1)} %get-tuple-element.229), channel_id=1, source_target_pairs={{8,0},{16,8},{24,16},{32,24},{40,32},{48,40},{56,48},{64,56},{72,6... | collective-permute-start | bytes 124424 | tf_op jit(solution)/shard_map/while/body/eval_jaxpr/ppermute | solution.py:48
  107.7 4.5 collective-permute-start.1
  112.4 12.7 %collective-permute-start.2 = (f32[27,18,24]{2,1,0:T(8,128)S(1)}, f32[27,18,24]{2,1,0:T(8,128)S(1)}, u32[]{:S(2)}, u32[]{:S(2)}) collective-permute-start(f32[27,18,24]{2,1,0:T(8,128)S(1)} %get-tuple-element.231), channel_id=1, source_target_pairs={{1,0},{2,1},{3,2},{4,3},{5,4},{6,5},{7,6},{9,8},{10,9},{11,10},{12... | collective-permute-start | bytes 139976 | tf_op jit(solution)/shard_map/while/body/eval_jaxpr/ppermute | solution.py:48
  113.7 19.7 %collective-permute-start.3 = (f32[27,18,24]{2,1,0:T(8,128)S(1)}, f32[27,18,24]{2,1,0:T(8,128)S(1)}, u32[]{:S(2)}, u32[]{:S(2)}) collective-permute-start(f32[27,18,24]{2,1,0:T(8,128)S(1)} %get-tuple-element.232), channel_id=1, source_target_pairs={{0,1},{1,2},{2,3},{3,4},{4,5},{5,6},{6,7},{8,9},{9,10},{10,11},{11... | collective-permute-start | bytes 139976 | tf_op jit(solution)/shard_map/while/body/eval_jaxpr/ppermute | solution.py:46
  134.2 1.1 copy-start
  138.0 5.6 %collective-permute-start = (f32[27,1,384]{2,1,0:T(1,128)S(1)}, f32[27,1,384]{2,1,0:T(1,128)S(1)}, u32[]{:S(2)}, u32[]{:S(2)}) collective-permute-start(f32[27,1,384]{2,1,0:T(1,128)S(1)} %get-tuple-element.229), channel_id=1, source_target_pairs={{8,0},{16,8},{24,16},{32,24},{40,32},{48,40},{56,48},{64,56},{72,6... | collective-permute-start | bytes 124424 | tf_op jit(solution)/shard_map/while/body/eval_jaxpr/ppermute | solution.py:48
  140.2 4.5 collective-permute-start.1
  144.9 12.7 %collective-permute-start.2 = (f32[27,18,24]{2,1,0:T(8,128)S(1)}, f32[27,18,24]{2,1,0:T(8,128)S(1)}, u32[]{:S(2)}, u32[]{:S(2)}) collective-permute-start(f32[27,18,24]{2,1,0:T(8,128)S(1)} %get-tuple-element.231), channel_id=1, source_target_pairs={{1,0},{2,1},{3,2},{4,3},{5,4},{6,5},{7,6},{9,8},{10,9},{11,10},{12... | collective-permute-start | bytes 139976 | tf_op jit(solution)/shard_map/while/body/eval_jaxpr/ppermute | solution.py:48
  146.2 19.7 %collective-permute-start.3 = (f32[27,18,24]{2,1,0:T(8,128)S(1)}, f32[27,18,24]{2,1,0:T(8,128)S(1)}, u32[]{:S(2)}, u32[]{:S(2)}) collective-permute-start(f32[27,18,24]{2,1,0:T(8,128)S(1)} %get-tuple-element.232), channel_id=1, source_target_pairs={{0,1},{1,2},{2,3},{3,4},{4,5},{5,6},{6,7},{8,9},{9,10},{10,11},{11... | collective-permute-start | bytes 139976 | tf_op jit(solution)/shard_map/while/body/eval_jaxpr/ppermute | solution.py:46
  166.7 1.1 copy-start
  170.5 5.6 %collective-permute-start = (f32[27,1,384]{2,1,0:T(1,128)S(1)}, f32[27,1,384]{2,1,0:T(1,128)S(1)}, u32[]{:S(2)}, u32[]{:S(2)}) collective-permute-start(f32[27,1,384]{2,1,0:T(1,128)S(1)} %get-tuple-element.229), channel_id=1, source_target_pairs={{8,0},{16,8},{24,16},{32,24},{40,32},{48,40},{56,48},{64,56},{72,6... | collective-permute-start | bytes 124424 | tf_op jit(solution)/shard_map/while/body/eval_jaxpr/ppermute | solution.py:48
  172.7 4.5 collective-permute-start.1
  177.4 12.7 %collective-permute-start.2 = (f32[27,18,24]{2,1,0:T(8,128)S(1)}, f32[27,18,24]{2,1,0:T(8,128)S(1)}, u32[]{:S(2)}, u32[]{:S(2)}) collective-permute-start(f32[27,18,24]{2,1,0:T(8,128)S(1)} %get-tuple-element.231), channel_id=1, source_target_pairs={{1,0},{2,1},{3,2},{4,3},{5,4},{6,5},{7,6},{9,8},{10,9},{11,10},{12... | collective-permute-start | bytes 139976 | tf_op jit(solution)/shard_map/while/body/eval_jaxpr/ppermute | solution.py:48
  178.7 19.3 %collective-permute-start.3 = (f32[27,18,24]{2,1,0:T(8,128)S(1)}, f32[27,18,24]{2,1,0:T(8,128)S(1)}, u32[]{:S(2)}, u32[]{:S(2)}) collective-permute-start(f32[27,18,24]{2,1,0:T(8,128)S(1)} %get-tuple-element.232), channel_id=1, source_target_pairs={{0,1},{1,2},{2,3},{3,4},{4,5},{5,6},{6,7},{8,9},{9,10},{10,11},{11... | collective-permute-start | bytes 139976 | tf_op jit(solution)/shard_map/while/body/eval_jaxpr/ppermute | solution.py:46
  198.8 1.1 copy-start
  202.6 7.4 %collective-permute-start = (f32[27,1,384]{2,1,0:T(1,128)S(1)}, f32[27,1,384]{2,1,0:T(1,128)S(1)}, u32[]{:S(2)}, u32[]{:S(2)}) collective-permute-start(f32[27,1,384]{2,1,0:T(1,128)S(1)} %get-tuple-element.229), channel_id=1, source_target_pairs={{8,0},{16,8},{24,16},{32,24},{40,32},{48,40},{56,48},{64,56},{72,6... | collective-permute-start | bytes 124424 | tf_op jit(solution)/shard_map/while/body/eval_jaxpr/ppermute | solution.py:48
  204.8 6.3 %collective-permute-start.1 = (f32[27,1,384]{2,1,0:T(1,128)S(1)}, f32[27,1,384]{2,1,0:T(1,128)S(1)}, u32[]{:S(2)}, u32[]{:S(2)}) collective-permute-start(f32[27,1,384]{2,1,0:T(1,128)S(1)} %get-tuple-element.230), channel_id=1, source_target_pairs={{0,8},{8,16},{16,24},{24,32},{32,40},{40,48},{48,56},{56,64},{64,7... | collective-permute-start | bytes 124424 | tf_op jit(solution)/shard_map/while/body/eval_jaxpr/ppermute | solution.py:46
  211.3 10.8 %collective-permute-start.2 = (f32[27,18,24]{2,1,0:T(8,128)S(1)}, f32[27,18,24]{2,1,0:T(8,128)S(1)}, u32[]{:S(2)}, u32[]{:S(2)}) collective-permute-start(f32[27,18,24]{2,1,0:T(8,128)S(1)} %get-tuple-element.231), channel_id=1, source_target_pairs={{1,0},{2,1},{3,2},{4,3},{5,4},{6,5},{7,6},{9,8},{10,9},{11,10},{12... | collective-permute-start | bytes 139976 | tf_op jit(solution)/shard_map/while/body/eval_jaxpr/ppermute | solution.py:48
  212.6 17.5 %collective-permute-start.3 = (f32[27,18,24]{2,1,0:T(8,128)S(1)}, f32[27,18,24]{2,1,0:T(8,128)S(1)}, u32[]{:S(2)}, u32[]{:S(2)}) collective-permute-start(f32[27,18,24]{2,1,0:T(8,128)S(1)} %get-tuple-element.232), channel_id=1, source_target_pairs={{0,1},{1,2},{2,3},{3,4},{4,5},{5,6},{6,7},{8,9},{9,10},{10,11},{11... | collective-permute-start | bytes 139976 | tf_op jit(solution)/shard_map/while/body/eval_jaxpr/ppermute | solution.py:46
  230.9 1.1 copy-start
  234.7 9.2 %collective-permute-start = (f32[27,1,384]{2,1,0:T(1,128)S(1)}, f32[27,1,384]{2,1,0:T(1,128)S(1)}, u32[]{:S(2)}, u32[]{:S(2)}) collective-permute-start(f32[27,1,384]{2,1,0:T(1,128)S(1)} %get-tuple-element.229), channel_id=1, source_target_pairs={{8,0},{16,8},{24,16},{32,24},{40,32},{48,40},{56,48},{64,56},{72,6... | collective-permute-start | bytes 124424 | tf_op jit(solution)/shard_map/while/body/eval_jaxpr/ppermute | solution.py:48
  236.8 8.2 %collective-permute-start.1 = (f32[27,1,384]{2,1,0:T(1,128)S(1)}, f32[27,1,384]{2,1,0:T(1,128)S(1)}, u32[]{:S(2)}, u32[]{:S(2)}) collective-permute-start(f32[27,1,384]{2,1,0:T(1,128)S(1)} %get-tuple-element.230), channel_id=1, source_target_pairs={{0,8},{8,16},{16,24},{24,32},{32,40},{40,48},{48,56},{56,64},{64,7... | collective-permute-start | bytes 124424 | tf_op jit(solution)/shard_map/while/body/eval_jaxpr/ppermute | solution.py:46
  245.2 10.1 %collective-permute-start.2 = (f32[27,18,24]{2,1,0:T(8,128)S(1)}, f32[27,18,24]{2,1,0:T(8,128)S(1)}, u32[]{:S(2)}, u32[]{:S(2)}) collective-permute-start(f32[27,18,24]{2,1,0:T(8,128)S(1)} %get-tuple-element.231), channel_id=1, source_target_pairs={{1,0},{2,1},{3,2},{4,3},{5,4},{6,5},{7,6},{9,8},{10,9},{11,10},{12... | collective-permute-start | bytes 139976 | tf_op jit(solution)/shard_map/while/body/eval_jaxpr/ppermute | solution.py:48
  246.5 15.5 %collective-permute-start.3 = (f32[27,18,24]{2,1,0:T(8,128)S(1)}, f32[27,18,24]{2,1,0:T(8,128)S(1)}, u32[]{:S(2)}, u32[]{:S(2)}) collective-permute-start(f32[27,18,24]{2,1,0:T(8,128)S(1)} %get-tuple-element.232), channel_id=1, source_target_pairs={{0,1},{1,2},{2,3},{3,4},{4,5},{5,6},{6,7},{8,9},{9,10},{10,11},{11... | collective-permute-start | bytes 139976 | tf_op jit(solution)/shard_map/while/body/eval_jaxpr/ppermute | solution.py:46
  262.8 1.1 copy-start
where the time goes:
time: 450 us; the launch traced here: 449 us
  blocking collectives  178 us (40%)
  starting transfers between devices  122 us (27%)
  waiting for transfers between devices  104 us (23%)
  other arithmetic  38.7 us (9%)
    psum x1, blocking collectives, body(): total = lax.psum(total, ('gz', 'gy'))  178 us
    ppermute x16, starting transfers between devices, with_halo(): lax.ppermute(tail, axis, [(i, (i + 1) % count) for i in range(ends)])  79 us
    ppermute x16, waiting for transfers between devices, with_halo(): lax.ppermute(tail, axis, [(i, (i + 1) % count) for i in range(ends)])  64.3 us
    ppermute x16, starting transfers between devices, with_halo(): lax.ppermute(head, axis, [((i + 1) % count, i) for i in range(ends)])  42.8 us
    ppermute x16, waiting for transfers between devices, with_halo(): lax.ppermute(head, axis, [((i + 1) % count, i) for i in range(ends)])  39.3 us
    while x416, other arithmetic  26.4 us
  transfers between devices with their start and end apart: 32, of which 24 were waited for; matrix products, arithmetic and copies ran while one was open for 0% of the time, Pallas kernels for 0%

commit v1 on v0

v1 whole, which is shorter than its diff:
```python
import numpy as np

import jax
import jax.numpy as jnp
from jax import lax
from jax.experimental import pallas as pl
from jax.experimental.pallas import tpu as pltpu
from jax.sharding import Mesh, PartitionSpec as P

NX = 24
STEPS = 8
HALO = STEPS
TAU_F = 0.52
TAU_G = 0.5376
LAT19 = [
    (0, 0, 0),
    (1, 0, 0),
    (-1, 0, 0),
    (0, 1, 0),
    (0, -1, 0),
    (0, 0, 1),
    (0, 0, -1),
    (1, 1, 0),
    (-1, -1, 0),
    (1, -1, 0),
    (-1, 1, 0),
    (1, 0, 1),
    (-1, 0, -1),
    (1, 0, -1),
    (-1, 0, 1),
    (0, 1, 1),
    (0, -1, -1),
    (0, 1, -1),
    (0, -1, 1),
]
WGT19 = [1.0 / 3.0] + [1.0 / 18.0] * 6 + [1.0 / 36.0] * 12
LAT7 = LAT19[:7]
WGT7 = [0.25] + [0.125] * 6
OPP = [LAT19.index(tuple(-v for v in c)) for c in LAT19]

KAPPA = -1.0 / (1.0 - TAU_F)
W2 = KAPPA / 36.0
OMG = 1.0 / TAU_G
LAMG = 1.0 - OMG
BIG = 1e30

NS = 8
XT = NX // 8
ROWS = 40


def shift_lanes(v, by):
    return pltpu.roll(v, by % 128, axis=1)


def tile(ref, chan, s, xt, cvec=(0, 0, 0)):
    v = ref[chan, s + 1 - cvec[1], pl.ds(8 + 8 * xt - cvec[0], 8), :]
    return shift_lanes(v, cvec[2]) if cvec[2] else v


def put(ref, chan, s, xt, v):
    ref[chan, s + 1, pl.ds(8 + 8 * xt, 8), :] = v


def wrap(ref, chan, low, high):
    for xt in range(XT):
        rows = pl.ds(8 + 8 * xt, 8)
        if low:
            ref[chan, 0, rows, :] = shift_lanes(ref[chan, NS, rows, :], 32)
        if high:
            ref[chan, NS + 1, rows, :] = shift_lanes(ref[chan, 1, rows, :], -32)


def moments(f):
    quad = []
    for k in (7, 11, 15):
        p, m = f[k] + f[k + 2], f[k + 1] + f[k + 3]
        quad.append((p + m, p - m, (f[k] - f[k + 2]) - (f[k + 1] - f[k + 3])))
    rho = f[0] + (f[1] + f[2]) + (f[3] + f[4]) + (f[5] + f[6])
    rho = rho + quad[0][0] + quad[1][0] + quad[2][0]
    mx = (f[1] - f[2]) + quad[0][1] + quad[1][1]
    my = (f[3] - f[4]) + quad[0][2] + quad[2][1]
    mz = (f[5] - f[6]) + quad[1][2] + quad[2][2]
    return rho, mx, my, mz


def inverse(v):
    r = pl.reciprocal(v, approx=True)
    return r * (2.0 - v * r)


def collide(f, g):
    rho, mx, my, mz = moments(f)
    inv = inverse(rho)
    mom = (mx, my, mz)
    u = [m * inv for m in mom]
    y = [(4.5 * W2) * m for m in mom]
    diag = [y[a] * u[a] for a in range(3)]
    o = [(3.0 * W2) * m for m in mom]
    base = W2 * rho - (diag[0] + diag[1] + diag[2]) * (1.0 / 3.0)
    t = [base + d for d in diag]
    post = [None] * 19
    post[0] = f[0] + 12.0 * base
    for a in range(3):
        e, od = t[a] + t[a], o[a] + o[a]
        post[1 + 2 * a] = f[1 + 2 * a] + (e + od)
        post[2 + 2 * a] = f[2 + 2 * a] + (e - od)
    for k, a, b in ((7, 0, 1), (11, 0, 2), (15, 1, 2)):
        e = t[a] + diag[b]
        cross = (y[a] + y[a]) * u[b]
        ep, em = e + cross, e - cross
        op, om = o[a] + o[b], o[a] - o[b]
        post[k] = f[k] + (ep + op)
        post[k + 1] = f[k + 1] + (ep - op)
        post[k + 2] = f[k + 2] + (em + om)
        post[k + 3] = f[k + 3] + (em - om)
    temp = g[0] + (g[1] + g[2]) + (g[3] + g[4]) + (g[5] + g[6])
    eq = (0.125 * OMG) * temp
    eq4 = (0.5 * OMG) * temp
    post.append(LAMG * g[0] + (eq + eq))
    for a in range(3):
        ua = eq4 * u[a]
        post.append(LAMG * g[1 + 2 * a] + (eq + ua))
        post.append(LAMG * g[2 + 2 * a] + (eq - ua))
    return post


def stream(src, wa, wb, s, xt):
    f = [tile(src, 0, s, xt)]
    g = [tile(src, 19, s, xt)]
    for i in range(1, 19):
        moved = tile(src, i, s, xt, LAT19[i])
        open_ = moved < BIG
        f.append(jnp.where(open_, moved, tile(src, OPP[i], s, xt)))
        if i < 7:
            back = tile(src, 19 + OPP[i], s, xt)
            coeff = pl.ds(8 * xt, 8)
            back = wa[i - 1, s, coeff, :] * back + wb[i - 1, s, coeff, :]
            g.append(jnp.where(open_, tile(src, 19 + i, s, xt, LAT19[i]), back))
    return f, g


def window(zbase, left, own, right, top, bot, temp_out, flow_out, part_out,
           stage, inp, kinds, pops, wa, wb, res):
    height = zbase[1]
    for a in range(5):
        blocks = (left[a], own[a, :, 0:192], own[a, :, 192:384], right[a])
        for q in range(4):
            r0 = 32 * q
            stage[a, r0 : r0 + 8, 0:192] = top[a, :, 192 * q : 192 * q + 192]
            stage[a, r0 + 8 : r0 + 24, 0:192] = blocks[q]
            stage[a, r0 + 24 : r0 + 32, 0:192] = bot[a, :, 192 * q : 192 * q + 192]
        inp[a, 0:16] = stage[a, :, 0:128].T.reshape(16, 8, 128)
        inp[a, 16:24] = stage[a, :, 128:256].T[0:64].reshape(8, 8, 128)

    lane = lax.broadcasted_iota(jnp.int32, (8, 128), 1)
    zin = lane % 32
    mine = (zin >= HALO) & (zin < 32 - HALO) & (lane >= 32) & (lane < 96)
    zpos = zbase[0] + zin.astype(jnp.float32)
    ramp = 0.5 - 0.75 * (zpos + 0.5) / height

    def first(s, carry):
        for xt in range(XT):
            kind = inp[0, s * XT + xt]
            put(kinds, 0, s, xt, kind)
            fluid = kind == 0.0
            u = [jnp.where(fluid, inp[2 + a, s * XT + xt], 0.0) for a in range(3)]
            walls = jnp.where(kind == 2.0, 0.5, jnp.where(kind == 3.0, -0.5, 0.0))
            temp = jnp.where(fluid, ramp + 0.05 * inp[1, s * XT + xt], walls)
            usq = u[0] * u[0] + u[1] * u[1] + u[2] * u[2]
            f, g = [], []
            for i in range(19):
                c = LAT19[i]
                if i == 0:
                    f.append(jnp.where(fluid, WGT19[0] * (1.0 - 1.5 * usq), jnp.nan))
                    g.append(WGT7[0] * temp)
                    continue
                proj = sum(u[a] if c[a] > 0 else -u[a] for a in range(3) if c[a])
                f.append(WGT19[i] * (1.0 + 3.0 * proj + 4.5 * proj * proj - 1.5 * usq))
                if i < 7:
                    g.append(WGT7[i] * temp * (1.0 + 4.0 * proj))
            for chan, v in enumerate(collide(f, g)):
                put(pops.at[0], chan, s, xt, v)
        return carry

    lax.fori_loop(0, NS, first, 0)
    wrap(kinds, 0, True, True)

    def edges(dst):
        for i in range(1, 19):
            if LAT19[i][1]:
                wrap(dst, i, LAT19[i][1] > 0, LAT19[i][1] < 0)
                if i < 7:
                    wrap(dst, 19 + i, LAT19[i][1] > 0, LAT19[i][1] < 0)

    edges(pops.at[0])

    def walls_of(s, carry):
        for xt in range(XT):
            rows = pl.ds(8 * xt, 8)
            for i in range(1, 7):
                near = tile(kinds, 0, s, xt, LAT19[i])
                hot, cold = near == 2.0, near == 3.0
                wa[i - 1, s, rows, :] = jnp.where(hot | cold, -1.0, 1.0)
                wb[i - 1, s, rows, :] = jnp.where(hot, 0.125, jnp.where(cold, -0.125, 0.0))
        return carry

    lax.fori_loop(0, NS, walls_of, 0)

    def step(k, carry):
        src, dst = pops.at[lax.rem(k + 1, 2)], pops.at[lax.rem(k, 2)]

        def line(s, c):
            for xt in range(XT):
                f, g = stream(src, wa, wb, s, xt)
                for chan, v in enumerate(collide(f, g)):
                    put(dst, chan, s, xt, v)
            return c

        lax.fori_loop(0, NS, line, 0)
        edges(dst)
        return carry

    lax.fori_loop(1, STEPS, step, 0)
    src = pops.at[(STEPS - 1) % 2]

    def last(s, total):
        for xt in range(XT):
            f, g = stream(src, wa, wb, s, xt)
            rho, mx, my, mz = moments(f)
            fluid = f[0] < BIG
            inv = inverse(rho)
            kind = tile(kinds, 0, s, xt)
            walls = jnp.where(kind == 2.0, 0.5, jnp.where(kind == 3.0, -0.5, 0.0))
            temp = g[0] + (g[1] + g[2]) + (g[3] + g[4]) + (g[5] + g[6])
            temp = jnp.where(fluid, temp, walls)
            res[0, s * XT + xt] = temp
            for a, m in enumerate((mx, my, mz)):
                res[1 + a, s * XT + xt] = jnp.where(fluid, m * inv, 0.0)
            heated = fluid & mine & (tile(kinds, 0, s, xt, (0, 1, 0)) == 2.0)
            total = total + jnp.where(heated, 0.5 - temp, 0.0)
        return total

    total = lax.fori_loop(0, NS, last, jnp.zeros((8, 128), jnp.float32))
    part_out[...] = jnp.full(part_out.shape, jnp.sum(total), jnp.float32)
    for o in range(4):
        one = res[o, 0:16].reshape(128, 128).T
        two = res[o, 16:32].reshape(128, 128).T
        for q in (1, 2):
            rows = slice(32 * q + 8, 32 * q + 24)
            at = 192 * (q - 1)
            val = jnp.concatenate([one[rows], two[rows, 0:64]], axis=1)
            if o == 0:
                temp_out[:, at : at + 192] = val
            else:
                flow_out[o - 1, :, at : at + 192] = val


def all_sum(part, axes, count):
    return jnp.sum(lax.all_to_all(part, axes, 0, 0, tiled=True), axis=0)


def make_body(gz, gy, near, far, n_near, n_far, n_gz, n_gy):
    def body(cell_type, perturb, velocity):
        slab, cells = cell_type.shape
        height = slab * n_gz
        own = jnp.concatenate(
            [
                cell_type.astype(jnp.float32)[None],
                perturb.astype(jnp.float32)[None],
                velocity,
            ]
        )
        rim = HALO * NX
        up = [(i, (i + 1) % n_gy) for i in range(n_gy)]
        down = [((i + 1) % n_gy, i) for i in range(n_gy)]
        left = lax.ppermute(own[:, :, cells - rim :], gy, up)
        right = lax.ppermute(own[:, :, :rim], gy, down)
        wide = jnp.concatenate([left, own, right], axis=2)
        up = [(i, (i + 1) % n_gz) for i in range(n_gz)]
        down = [((i + 1) % n_gz, i) for i in range(n_gz)]
        top = lax.ppermute(wide[:, slab - HALO :], gz, up)
        bot = lax.ppermute(wide[:, :HALO], gz, down)
        zbase = jnp.stack(
            [
                (lax.axis_index(gz) * slab - HALO).astype(jnp.float32),
                jnp.float32(height),
            ]
        )
        vmem = pl.BlockSpec(memory_space=pltpu.VMEM)
        f32 = jnp.float32
        temp, flow, part = pl.pallas_call(
            window,
            in_specs=[pl.BlockSpec(memory_space=pltpu.SMEM)] + [vmem] * 5,
            out_specs=[vmem] * 3,
            out_shape=[
                jax.ShapeDtypeStruct((slab, cells), f32),
                jax.ShapeDtypeStruct((3, slab, cells), f32),
                jax.ShapeDtypeStruct((n_near, 128), f32),
            ],
            scratch_shapes=[
                pltpu.VMEM((5, 128, 256), f32),
                pltpu.VMEM((5, NS * XT, 8, 128), f32),
                pltpu.VMEM((1, NS + 2, ROWS, 128), f32),
                pltpu.VMEM((2, 26, NS + 2, ROWS, 128), f32),
                pltpu.VMEM((6, NS, NX, 128), f32),
                pltpu.VMEM((6, NS, NX, 128), f32),
                pltpu.VMEM((4, 32, 8, 128), f32),
            ],
            compiler_params=pltpu.CompilerParams(vmem_limit_bytes=40 * 1024 * 1024),
            name="lattice_window",
        )(zbase, left, own, right, top, bot)
        line = all_sum(part, near, n_near)
        line = all_sum(jnp.broadcast_to(line, (n_far, 128)), far, n_far)
        return temp, flow, line[0] * (2.0 / (NX * height))

    return body


def solution(mesh):
    n_gz, n_gy = mesh.shape["gz"], mesh.shape["gy"]
    z = n_gz // 4
    fine = Mesh(
        np.asarray(mesh.devices).reshape(2, z, 2, n_gy),
        ("yl", "z", "core", "gy"),
    )
    gz = ("yl", "z", "core")
    near = ("yl", "core", "gy")
    body = make_body(gz, "gy", near, "z", 4 * n_gy, z, n_gz, n_gy)
    return jax.shard_map(
        body,
        mesh=fine,
        in_specs=(P(gz, "gy"), P(gz, "gy"), P(None, gz, "gy")),
        out_specs=(P(gz, "gy"), P(None, gz, "gy"), P()),
        check_vma=False,
    )
```

time: 450 us -> 114 us (0.25)
  blocking collectives: 178 us -> 56.6 us
  waiting for transfers between devices: 104 us -> 3.43 us
  starting transfers between devices: 122 us -> 26.9 us
  other arithmetic: 38.7 us -> 1.08 us
  Pallas kernels: 0 us -> 23.4 us
    psum x1 -> x0, blocking collectives: 178 us -> none  [body(): total = lax.psum(total, ('gz', 'gy'))]
    ppermute x32 -> x4, waiting for transfers between devices: 104 us -> 3.43 us  [the longest x1 2.56 us: body(): right = lax.ppermute(own[:, :, :rim], gy, down)]
    ppermute x32 -> x4, starting transfers between devices: 122 us -> 26.9 us  [the longest x1 11.6 us: body(): bot = lax.ppermute(wide[:, :HALO], gz, down)]
    all_to_all x0 -> x2, blocking collectives: none -> 56.6 us  [all_sum(): return jnp.sum(lax.all_to_all(part, axes, 0, 0, tiled=True), axis=0)]
    while x416 -> x0, other arithmetic: 26.4 us -> none
    pallas_call x0 -> x1, Pallas kernels: none -> 23.4 us  [body(): pl.pallas_call(window, in_specs=[pl.BlockSpec(memory_space=pltpu.SMEM)] +...]
    concatenate x8 -> x2, other arithmetic: 6.56 us -> 0.14 us  [the longest x1 0.13 us: body(): wide = jnp.concatenate([left, own, right], axis=2)]
  transfers between devices with their start and end apart: 32 -> 4, of which waited for: 24 -> 2; matrix products, arithmetic and copies ran while one was open for 0% -> 0% of each run, Pallas kernels for 0% -> 0%
where the time goes in v1:
time: 114 us; the launch traced here: 113 us
  blocking collectives  56.6 us (50%)
  starting transfers between devices  26.9 us (24%)
  Pallas kernels  23.4 us (21%)
  waiting for transfers between devices  3.43 us (3%)
  between operations  1.88 us (2%)
    all_to_all x2, blocking collectives, all_sum(): return jnp.sum(lax.all_to_all(part, axes, 0, 0, tiled=True), axis=0)  56.6 us
    pallas_call x1, Pallas kernels, body(): pl.pallas_call(window, in_specs=[pl.BlockSpec(memory_space=pltpu.SMEM)] +...  23.4 us
    ppermute x1, starting transfers between devices, body(): bot = lax.ppermute(wide[:, :HALO], gz, down)  11.6 us
    ppermute x1, starting transfers between devices, body(): left = lax.ppermute(own[:, :, cells - rim:], gy, up)  5.65 us
    ppermute x1, starting transfers between devices, body(): top = lax.ppermute(wide[:, slab - HALO:], gz, up)  5.54 us
    ppermute x1, starting transfers between devices, body(): right = lax.ppermute(own[:, :, :rim], gy, down)  4.12 us
    ppermute x1, waiting for transfers between devices, body(): right = lax.ppermute(own[:, :, :rim], gy, down)  2.56 us
  transfers between devices with their start and end apart: 4, of which 2 were waited for; matrix products, arithmetic and copies ran while one was open for 0% of the time, Pallas kernels for 0%

profile of v1, /device:TPU:1, one launch (start us, length us, event | category | flops | bytes accessed | tf_op | source)
XLA Modules:
  0.0 113.5 jit_solution(10492845414705728140)
XLA Ops:
  0.6 0.0 copy-start
  0.6 0.8 convert_bitcast_fusion
  1.4 0.1 copy-done
  1.5 0.1 fusion.1
  1.6 5.7 %collective-permute-start = (f32[5,16,192]{2,1,0:T(8,128)S(1)}, f32[5,16,192]{2,1,0:T(8,128)S(1)}, u32[]{:S(2)}, u32[]{:S(2)}) collective-permute-start(f32[5,16,192]{2,1,0:T(8,128)S(1)} %get-tuple-element.12), channel_id=1, source_target_pairs={{0,1},{1,2},{2,3},{3,4},{4,5},{5,6},{6,7},{7,0},{8,9},{9,10},{10,1... | collective-permute-start | bytes 184328 | tf_op jit(solution)/shard_map/ppermute | solution.py:277
  7.3 4.1 %collective-permute-start.1 = (f32[5,16,192]{2,1,0:T(8,128)S(1)}, f32[5,16,192]{2,1,0:T(8,128)S(1)}, u32[]{:S(2)}, u32[]{:S(2)}) collective-permute-start(f32[5,16,192]{2,1,0:T(8,128)S(1)} %get-tuple-element.11), channel_id=1, source_target_pairs={{1,0},{2,1},{3,2},{4,3},{5,4},{6,5},{7,6},{0,7},{9,8},{10,9},{11,1... | collective-permute-start | bytes 184328 | tf_op jit(solution)/shard_map/ppermute | solution.py:278
  11.4 0.0 collective-permute-done.left
  11.4 2.6 %collective-permute-done.1.right = f32[5,16,192]{2,1,0:T(8,128)S(1)} collective-permute-done((f32[5,16,192]{2,1,0:T(8,128)S(1)}, f32[5,16,192]{2,1,0:T(8,128)S(1)}, u32[]{:S(2)}, u32[]{:S(2)}) %collective-permute-start.1) | collective-permute-done | bytes 61472 | tf_op jit(solution)/shard_map/ppermute | solution.py:278
  14.0 0.1 pad_maximum_fusion
  14.1 5.5 %collective-permute-start.2 = (f32[5,8,768]{2,1,0:T(8,128)S(1)}, f32[5,8,768]{2,1,0:T(8,128)S(1)}, u32[]{:S(2)}, u32[]{:S(2)}) collective-permute-start(f32[5,8,768]{2,1,0:T(8,128)S(1)} %get-tuple-element.10), channel_id=1, source_target_pairs={{0,8},{8,16},{16,24},{24,32},{32,40},{40,48},{48,56},{56,64},{64,7... | collective-permute-start | bytes 368648 | tf_op jit(solution)/shard_map/ppermute | solution.py:282
  19.7 11.6 %collective-permute-start.3 = (f32[5,8,768]{2,1,0:T(8,128)S(1)}, f32[5,8,768]{2,1,0:T(8,128)S(1)}, u32[]{:S(2)}, u32[]{:S(2)}) collective-permute-start(f32[5,8,768]{2,1,0:T(8,128)S(1)} %get-tuple-element.9), channel_id=1, source_target_pairs={{8,0},{16,8},{24,16},{32,24},{40,32},{48,40},{56,48},{64,56},{72,6... | collective-permute-start | bytes 368648 | tf_op jit(solution)/shard_map/ppermute | solution.py:283
  31.3 0.1 pad_maximum_fusion.2.zbase
  31.4 0.0 collective-permute-done.2.top
  31.4 0.9 collective-permute-done.3.bot
  32.2 23.4 %lattice_window.1 = (f32[16,384]{1,0:T(8,128)}, f32[3,16,384]{2,1,0:T(8,128)}, f32[32,128]{1,0:T(8,128)S(1)}) custom-call(f32[2]{0:T(128)S(1)} %pad_maximum_fusion.2.zbase, f32[5,16,192]{2,1,0:T(8,128)S(1)} %collective-permute-done.left, f32[5,16,384]{2,1,0:T(8,128)S(1)} %pad_maximum_fusion.1.own, f32[5,16,192]{2,1,0:T(8,128)S(1)} %collective-permute-done.1.right, ...), custom_call_target="tpu_custom_call" | custom-call | tf_op jit(solution)/shard_map/lattice_window/pallas_call | solution.py:292
  55.7 19.5 %all_to_all.15 = f32[32,1,128]{2,1,0:T(1,128)S(1)} all-to-all(f32[32,1,128]{2,1,0:T(1,128)S(1)} %bitcast.11), channel_id=1, replica_groups=mesh['yl'=2,'z'=32,'core'=2,'gy'=8] {'yl','core','gy'}, dimensions={0} | all-to-all | bytes 32768 | tf_op jit(solution)/shard_map/all_to_all | solution.py:260
  75.1 0.1 reduce_sum.18
  75.2 37.1 %all_to_all.16 = f32[32,1,128]{2,1,0:T(1,128)S(1)} all-to-all(f32[32,1,128]{2,1,0:T(1,128)S(1)} %broadcast_in_dim.11), channel_id=1, replica_groups=mesh['yl'=2,'z'=32,'core'=2,'gy'=8] {'z'}, dimensions={0} | all-to-all | bytes 32768 | tf_op jit(solution)/shard_map/all_to_all | solution.py:260
  (4 shorter events, 0.1 us)
Async XLA Ops:
  0.6 0.9 copy-start
  1.6 9.8 %collective-permute-start = (f32[5,16,192]{2,1,0:T(8,128)S(1)}, f32[5,16,192]{2,1,0:T(8,128)S(1)}, u32[]{:S(2)}, u32[]{:S(2)}) collective-permute-start(f32[5,16,192]{2,1,0:T(8,128)S(1)} %get-tuple-element.12), channel_id=1, source_target_pairs={{0,1},{1,2},{2,3},{3,4},{4,5},{5,6},{6,7},{7,0},{8,9},{9,10},{10,1... | collective-permute-start | bytes 184328 | tf_op jit(solution)/shard_map/ppermute | solution.py:277
  7.3 6.7 %collective-permute-start.1 = (f32[5,16,192]{2,1,0:T(8,128)S(1)}, f32[5,16,192]{2,1,0:T(8,128)S(1)}, u32[]{:S(2)}, u32[]{:S(2)}) collective-permute-start(f32[5,16,192]{2,1,0:T(8,128)S(1)} %get-tuple-element.11), channel_id=1, source_target_pairs={{1,0},{2,1},{3,2},{4,3},{5,4},{6,5},{7,6},{0,7},{9,8},{10,9},{11,1... | collective-permute-start | bytes 184328 | tf_op jit(solution)/shard_map/ppermute | solution.py:278
  14.1 17.2 %collective-permute-start.2 = (f32[5,8,768]{2,1,0:T(8,128)S(1)}, f32[5,8,768]{2,1,0:T(8,128)S(1)}, u32[]{:S(2)}, u32[]{:S(2)}) collective-permute-start(f32[5,8,768]{2,1,0:T(8,128)S(1)} %get-tuple-element.10), channel_id=1, source_target_pairs={{0,8},{8,16},{16,24},{24,32},{32,40},{40,48},{48,56},{56,64},{64,7... | collective-permute-start | bytes 368648 | tf_op jit(solution)/shard_map/ppermute | solution.py:282
  19.7 12.6 %collective-permute-start.3 = (f32[5,8,768]{2,1,0:T(8,128)S(1)}, f32[5,8,768]{2,1,0:T(8,128)S(1)}, u32[]{:S(2)}, u32[]{:S(2)}) collective-permute-start(f32[5,8,768]{2,1,0:T(8,128)S(1)} %get-tuple-element.9), channel_id=1, source_target_pairs={{8,0},{16,8},{24,16},{32,24},{40,32},{48,40},{56,48},{64,56},{72,6... | collective-permute-start | bytes 368648 | tf_op jit(solution)/shard_map/ppermute | solution.py:283

commit v2 on v1

--- a/solution.py
+++ b/solution.py
@@ -40,6 +40,7 @@
 
 KAPPA = -1.0 / (1.0 - TAU_F)
 W2 = KAPPA / 36.0
+KAPPA_0 = 1.0 / 36.0 / (1.0 - 1.0 / TAU_F)
 OMG = 1.0 / TAU_G
 LAMG = 1.0 - OMG
 BIG = 1e30
@@ -49,26 +50,59 @@
 ROWS = 40
 
 
+COPY = list(range(26))
+for _i in range(1, 19):
+    if LAT19[_i][2]:
+        COPY[_i] = 26 + sum(1 for c in COPY if c >= 26)
+for _i in range(1, 7):
+    if LAT19[_i][2]:
+        COPY[19 + _i] = 26 + sum(1 for c in COPY if c >= 26)
+NCHAN = 26 + sum(1 for c in COPY if c >= 26)
+
+
 def shift_lanes(v, by):
     return pltpu.roll(v, by % 128, axis=1)
 
 
-def tile(ref, chan, s, xt, cvec=(0, 0, 0)):
-    v = ref[chan, s + 1 - cvec[1], pl.ds(8 + 8 * xt - cvec[0], 8), :]
-    return shift_lanes(v, cvec[2]) if cvec[2] else v
-
-
-def put(ref, chan, s, xt, v):
-    ref[chan, s + 1, pl.ds(8 + 8 * xt, 8), :] = v
-
-
-def wrap(ref, chan, low, high):
+def velocity_of(chan):
+    return LAT19[chan] if chan < 19 else LAT19[chan - 19]
+
+
+def put(ref, chan, slot, xt, v):
+    ref[chan, slot, pl.ds(8 + 8 * xt, 8), :] = v
+
+
+def tile(ref, chan, s, xt):
+    return ref[chan, s + 1, pl.ds(8 + 8 * xt, 8), :]
+
+
+def moved_tile(ref, chan, s, xt):
+    c = velocity_of(chan)
+    return ref[COPY[chan], s + 1 - c[1], pl.ds(8 + 8 * xt - c[0], 8), :]
+
+
+def put_all(ref, s, xt, post):
+    for chan, v in enumerate(post):
+        put(ref, chan, s + 1, xt, v)
+
+
+def copies(ref):
+    def roll_line(s, carry):
+        for xt in range(XT):
+            for chan in range(26):
+                c = velocity_of(chan)
+                if c[2]:
+                    put(ref, COPY[chan], s + 1, xt, shift_lanes(tile(ref, chan, s, xt), c[2]))
+        return carry
+
     for xt in range(XT):
-        rows = pl.ds(8 + 8 * xt, 8)
-        if low:
-            ref[chan, 0, rows, :] = shift_lanes(ref[chan, NS, rows, :], 32)
-        if high:
-            ref[chan, NS + 1, rows, :] = shift_lanes(ref[chan, 1, rows, :], -32)
+        for chan in range(26):
+            c = velocity_of(chan)
+            if c[1] > 0:
+                put(ref, COPY[chan], 0, xt, shift_lanes(tile(ref, chan, NS - 1, xt), c[2] + 32))
+            if c[1] < 0:
+                put(ref, COPY[chan], NS + 1, xt, shift_lanes(tile(ref, chan, 0, xt), c[2] - 32))
+    lax.fori_loop(0, NS, roll_line, 0, unroll=True)
 
 
 def moments(f):
@@ -125,18 +159,38 @@
     return post
 
 
+def equilibrium(u):
+    y = [(4.5 * KAPPA_0) * v for v in u]
+    diag = [y[a] * u[a] for a in range(3)]
+    o = [(3.0 * KAPPA_0) * v for v in u]
+    base = KAPPA_0 - (diag[0] + diag[1] + diag[2]) * (1.0 / 3.0)
+    t = [base + d for d in diag]
+    f = [None] * 19
+    f[0] = 12.0 * base
+    for a in range(3):
+        e, od = t[a] + t[a], o[a] + o[a]
+        f[1 + 2 * a], f[2 + 2 * a] = e + od, e - od
+    for k, a, b in ((7, 0, 1), (11, 0, 2), (15, 1, 2)):
+        e = t[a] + diag[b]
+        cross = (y[a] + y[a]) * u[b]
+        ep, em = e + cross, e - cross
+        op, om = o[a] + o[b], o[a] - o[b]
+        f[k], f[k + 1], f[k + 2], f[k + 3] = ep + op, ep - op, em + om, em - om
+    return f
+
+
 def stream(src, wa, wb, s, xt):
     f = [tile(src, 0, s, xt)]
     g = [tile(src, 19, s, xt)]
     for i in range(1, 19):
-        moved = tile(src, i, s, xt, LAT19[i])
+        moved = moved_tile(src, i, s, xt)
         open_ = moved < BIG
         f.append(jnp.where(open_, moved, tile(src, OPP[i], s, xt)))
         if i < 7:
             back = tile(src, 19 + OPP[i], s, xt)
             coeff = pl.ds(8 * xt, 8)
             back = wa[i - 1, s, coeff, :] * back + wb[i - 1, s, coeff, :]
-            g.append(jnp.where(open_, tile(src, 19 + i, s, xt, LAT19[i]), back))
+            g.append(jnp.where(open_, moved_tile(src, 19 + i, s, xt), back))
     return f, g
 
 
@@ -162,50 +216,41 @@
     def first(s, carry):
         for xt in range(XT):
             kind = inp[0, s * XT + xt]
-            put(kinds, 0, s, xt, kind)
+            put(kinds, 0, s + 1, xt, kind)
+            put(kinds, 1, s + 1, xt, shift_lanes(kind, 1))
+            put(kinds, 2, s + 1, xt, shift_lanes(kind, -1))
             fluid = kind == 0.0
-            u = [jnp.where(fluid, inp[2 + a, s * XT + xt], 0.0) for a in range(3)]
-            walls = jnp.where(kind == 2.0, 0.5, jnp.where(kind == 3.0, -0.5, 0.0))
-            temp = jnp.where(fluid, ramp + 0.05 * inp[1, s * XT + xt], walls)
-            usq = u[0] * u[0] + u[1] * u[1] + u[2] * u[2]
-            f, g = [], []
-            for i in range(19):
-                c = LAT19[i]
-                if i == 0:
-                    f.append(jnp.where(fluid, WGT19[0] * (1.0 - 1.5 * usq), jnp.nan))
-                    g.append(WGT7[0] * temp)
-                    continue
-                proj = sum(u[a] if c[a] > 0 else -u[a] for a in range(3) if c[a])
-                f.append(WGT19[i] * (1.0 + 3.0 * proj + 4.5 * proj * proj - 1.5 * usq))
-                if i < 7:
-                    g.append(WGT7[i] * temp * (1.0 + 4.0 * proj))
-            for chan, v in enumerate(collide(f, g)):
-                put(pops.at[0], chan, s, xt, v)
+            u = [inp[2 + a, s * XT + xt] for a in range(3)]
+            temp = ramp + 0.05 * inp[1, s * XT + xt]
+            f = equilibrium(u)
+            f = [jnp.where(fluid, v, jnp.nan) for v in f]
+            eq, eq4 = 0.125 * temp, 0.5 * temp
+            f.append(eq + eq)
+            for a in range(3):
+                ua = eq4 * u[a]
+                f.append(eq + ua)
+                f.append(eq - ua)
+            put_all(pops.at[0], s, xt, f)
         return carry
 
-    lax.fori_loop(0, NS, first, 0)
-    wrap(kinds, 0, True, True)
-
-    def edges(dst):
-        for i in range(1, 19):
-            if LAT19[i][1]:
-                wrap(dst, i, LAT19[i][1] > 0, LAT19[i][1] < 0)
-                if i < 7:
-                    wrap(dst, 19 + i, LAT19[i][1] > 0, LAT19[i][1] < 0)
-
-    edges(pops.at[0])
+    lax.fori_loop(0, NS, first, 0, unroll=True)
+    copies(pops.at[0])
+    for xt in range(XT):
+        put(kinds, 0, NS + 1, xt, shift_lanes(tile(kinds, 0, 0, xt), -32))
+        put(kinds, 0, 0, xt, shift_lanes(tile(kinds, 0, NS - 1, xt), 32))
 
     def walls_of(s, carry):
         for xt in range(XT):
             rows = pl.ds(8 * xt, 8)
             for i in range(1, 7):
-                near = tile(kinds, 0, s, xt, LAT19[i])
+                c = LAT19[i]
+                near = kinds[(0, 1, 2)[c[2]], s + 1 - c[1], pl.ds(8 + 8 * xt - c[0], 8), :]
                 hot, cold = near == 2.0, near == 3.0
                 wa[i - 1, s, rows, :] = jnp.where(hot | cold, -1.0, 1.0)
                 wb[i - 1, s, rows, :] = jnp.where(hot, 0.125, jnp.where(cold, -0.125, 0.0))
         return carry
 
-    lax.fori_loop(0, NS, walls_of, 0)
+    lax.fori_loop(0, NS, walls_of, 0, unroll=True)
 
     def step(k, carry):
         src, dst = pops.at[lax.rem(k + 1, 2)], pops.at[lax.rem(k, 2)]
@@ -213,12 +258,11 @@
         def line(s, c):
             for xt in range(XT):
                 f, g = stream(src, wa, wb, s, xt)
-                for chan, v in enumerate(collide(f, g)):
-                    put(dst, chan, s, xt, v)
+                put_all(dst, s, xt, collide(f, g))
             return c
 
-        lax.fori_loop(0, NS, line, 0)
-        edges(dst)
+        lax.fori_loop(0, NS, line, 0, unroll=4)
+        copies(dst)
         return carry
 
     lax.fori_loop(1, STEPS, step, 0)
@@ -237,11 +281,11 @@
             res[0, s * XT + xt] = temp
             for a, m in enumerate((mx, my, mz)):
                 res[1 + a, s * XT + xt] = jnp.where(fluid, m * inv, 0.0)
-            heated = fluid & mine & (tile(kinds, 0, s, xt, (0, 1, 0)) == 2.0)
+            heated = fluid & mine & (kinds[0, s, pl.ds(8 + 8 * xt, 8), :] == 2.0)
             total = total + jnp.where(heated, 0.5 - temp, 0.0)
         return total
 
-    total = lax.fori_loop(0, NS, last, jnp.zeros((8, 128), jnp.float32))
+    total = lax.fori_loop(0, NS, last, jnp.zeros((8, 128), jnp.float32), unroll=True)
     part_out[...] = jnp.full(part_out.shape, jnp.sum(total), jnp.float32)
     for o in range(4):
         one = res[o, 0:16].reshape(128, 128).T
@@ -254,6 +298,17 @@
                 temp_out[:, at : at + 192] = val
             else:
                 flow_out[o - 1, :, at : at + 192] = val
+
+
+SCRATCH = [
+    pltpu.VMEM((5, 128, 256), jnp.float32),
+    pltpu.VMEM((5, NS * XT, 8, 128), jnp.float32),
+    pltpu.VMEM((3, NS + 2, ROWS, 128), jnp.float32),
+    pltpu.VMEM((2, NCHAN, NS + 2, ROWS, 128), jnp.float32),
+    pltpu.VMEM((6, NS, NX, 128), jnp.float32),
+    pltpu.VMEM((6, NS, NX, 128), jnp.float32),
+    pltpu.VMEM((4, 32, 8, 128), jnp.float32),
+]
 
 
 def all_sum(part, axes, count):
@@ -298,15 +353,7 @@
                 jax.ShapeDtypeStruct((3, slab, cells), f32),
                 jax.ShapeDtypeStruct((n_near, 128), f32),
             ],
-            scratch_shapes=[
-                pltpu.VMEM((5, 128, 256), f32),
-                pltpu.VMEM((5, NS * XT, 8, 128), f32),
-                pltpu.VMEM((1, NS + 2, ROWS, 128), f32),
-                pltpu.VMEM((2, 26, NS + 2, ROWS, 128), f32),
-                pltpu.VMEM((6, NS, NX, 128), f32),
-                pltpu.VMEM((6, NS, NX, 128), f32),
-                pltpu.VMEM((4, 32, 8, 128), f32),
-            ],
+            scratch_shapes=SCRATCH,
             compiler_params=pltpu.CompilerParams(vmem_limit_bytes=40 * 1024 * 1024),
             name="lattice_window",
         )(zbase, left, own, right, top, bot)

time: 114 us -> 103 us (0.904)
  Pallas kernels: 23.4 us -> 12.4 us
    pallas_call x1, Pallas kernels: 23.4 us -> 12.4 us  [body(): pl.pallas_call(window, in_specs=[pl.BlockSpec(memory_space=pltpu.SMEM)] +...]
where the time goes in v2:
time: 103 us; the launch traced here: 102 us
  blocking collectives  56.6 us (55%)
  starting transfers between devices  26.9 us (26%)
  Pallas kernels  12.4 us (12%)
  waiting for transfers between devices  3.43 us (3%)
  between operations  1.88 us (2%)
  other arithmetic  1.08 us (1%)
    all_to_all x2, blocking collectives, all_sum(): return jnp.sum(lax.all_to_all(part, axes, 0, 0, tiled=True), axis=0)  56.6 us
    pallas_call x1, Pallas kernels, body(): pl.pallas_call(window, in_specs=[pl.BlockSpec(memory_space=pltpu.SMEM)] +...  12.4 us
    ppermute x1, starting transfers between devices, body(): bot = lax.ppermute(wide[:, :HALO], gz, down)  11.6 us
    ppermute x1, starting transfers between devices, body(): left = lax.ppermute(own[:, :, cells - rim:], gy, up)  5.65 us
    ppermute x1, starting transfers between devices, body(): top = lax.ppermute(wide[:, slab - HALO:], gz, up)  5.54 us
    ppermute x1, starting transfers between devices, body(): right = lax.ppermute(own[:, :, :rim], gy, down)  4.12 us
    ppermute x1, waiting for transfers between devices, body(): right = lax.ppermute(own[:, :, :rim], gy, down)  2.56 us
  transfers between devices with their start and end apart: 4, of which 2 were waited for; matrix products, arithmetic and copies ran while one was open for 0% of the time, Pallas kernels for 0%

profile of v2, /device:TPU:1, one launch (start us, length us, event | category | flops | bytes accessed | tf_op | source)
XLA Modules:
  0.0 102.4 jit_solution(2693677232445616963)
XLA Ops:
  0.6 0.0 copy-start
  0.6 0.8 convert_bitcast_fusion
  1.4 0.1 copy-done
  1.5 0.1 fusion.1
  1.6 5.7 %collective-permute-start = (f32[5,16,192]{2,1,0:T(8,128)S(1)}, f32[5,16,192]{2,1,0:T(8,128)S(1)}, u32[]{:S(2)}, u32[]{:S(2)}) collective-permute-start(f32[5,16,192]{2,1,0:T(8,128)S(1)} %get-tuple-element.12), channel_id=1, source_target_pairs={{0,1},{1,2},{2,3},{3,4},{4,5},{5,6},{6,7},{7,0},{8,9},{9,10},{10,1... | collective-permute-start | bytes 184328 | tf_op jit(solution)/shard_map/ppermute | solution.py:332
  7.3 4.1 %collective-permute-start.1 = (f32[5,16,192]{2,1,0:T(8,128)S(1)}, f32[5,16,192]{2,1,0:T(8,128)S(1)}, u32[]{:S(2)}, u32[]{:S(2)}) collective-permute-start(f32[5,16,192]{2,1,0:T(8,128)S(1)} %get-tuple-element.11), channel_id=1, source_target_pairs={{1,0},{2,1},{3,2},{4,3},{5,4},{6,5},{7,6},{0,7},{9,8},{10,9},{11,1... | collective-permute-start | bytes 184328 | tf_op jit(solution)/shard_map/ppermute | solution.py:333
  11.4 0.0 collective-permute-done.left
  11.4 2.6 %collective-permute-done.1.right = f32[5,16,192]{2,1,0:T(8,128)S(1)} collective-permute-done((f32[5,16,192]{2,1,0:T(8,128)S(1)}, f32[5,16,192]{2,1,0:T(8,128)S(1)}, u32[]{:S(2)}, u32[]{:S(2)}) %collective-permute-start.1) | collective-permute-done | bytes 61472 | tf_op jit(solution)/shard_map/ppermute | solution.py:333
  14.0 0.1 pad_maximum_fusion
  14.1 5.5 %collective-permute-start.2 = (f32[5,8,768]{2,1,0:T(8,128)S(1)}, f32[5,8,768]{2,1,0:T(8,128)S(1)}, u32[]{:S(2)}, u32[]{:S(2)}) collective-permute-start(f32[5,8,768]{2,1,0:T(8,128)S(1)} %get-tuple-element.10), channel_id=1, source_target_pairs={{0,8},{8,16},{16,24},{24,32},{32,40},{40,48},{48,56},{56,64},{64,7... | collective-permute-start | bytes 368648 | tf_op jit(solution)/shard_map/ppermute | solution.py:337
  19.7 11.6 %collective-permute-start.3 = (f32[5,8,768]{2,1,0:T(8,128)S(1)}, f32[5,8,768]{2,1,0:T(8,128)S(1)}, u32[]{:S(2)}, u32[]{:S(2)}) collective-permute-start(f32[5,8,768]{2,1,0:T(8,128)S(1)} %get-tuple-element.9), channel_id=1, source_target_pairs={{8,0},{16,8},{24,16},{32,24},{40,32},{48,40},{56,48},{64,56},{72,6... | collective-permute-start | bytes 368648 | tf_op jit(solution)/shard_map/ppermute | solution.py:338
  31.3 0.1 pad_maximum_fusion.2.zbase
  31.4 0.0 collective-permute-done.2.top
  31.4 0.9 collective-permute-done.3.bot
  32.2 12.4 %lattice_window.1 = (f32[16,384]{1,0:T(8,128)}, f32[3,16,384]{2,1,0:T(8,128)}, f32[32,128]{1,0:T(8,128)S(1)}) custom-call(f32[2]{0:T(128)S(1)} %pad_maximum_fusion.2.zbase, f32[5,16,192]{2,1,0:T(8,128)S(1)} %collective-permute-done.left, f32[5,16,384]{2,1,0:T(8,128)S(1)} %pad_maximum_fusion.1.own, f32[5,16,192]{2,1,0:T(8,128)S(1)} %collective-permute-done.1.right, ...), custom_call_target="tpu_custom_call" | custom-call | tf_op jit(solution)/shard_map/lattice_window/pallas_call | solution.py:347
  44.6 19.5 %all_to_all.15 = f32[32,1,128]{2,1,0:T(1,128)S(1)} all-to-all(f32[32,1,128]{2,1,0:T(1,128)S(1)} %bitcast.11), channel_id=1, replica_groups=mesh['yl'=2,'z'=32,'core'=2,'gy'=8] {'yl','core','gy'}, dimensions={0} | all-to-all | bytes 32768 | tf_op jit(solution)/shard_map/all_to_all | solution.py:315
  64.1 0.1 reduce_sum.18
  64.1 37.1 %all_to_all.16 = f32[32,1,128]{2,1,0:T(1,128)S(1)} all-to-all(f32[32,1,128]{2,1,0:T(1,128)S(1)} %broadcast_in_dim.11), channel_id=1, replica_groups=mesh['yl'=2,'z'=32,'core'=2,'gy'=8] {'z'}, dimensions={0} | all-to-all | bytes 32768 | tf_op jit(solution)/shard_map/all_to_all | solution.py:315
  (4 shorter events, 0.1 us)
Async XLA Ops:
  0.6 0.9 copy-start
  1.6 9.8 %collective-permute-start = (f32[5,16,192]{2,1,0:T(8,128)S(1)}, f32[5,16,192]{2,1,0:T(8,128)S(1)}, u32[]{:S(2)}, u32[]{:S(2)}) collective-permute-start(f32[5,16,192]{2,1,0:T(8,128)S(1)} %get-tuple-element.12), channel_id=1, source_target_pairs={{0,1},{1,2},{2,3},{3,4},{4,5},{5,6},{6,7},{7,0},{8,9},{9,10},{10,1... | collective-permute-start | bytes 184328 | tf_op jit(solution)/shard_map/ppermute | solution.py:332
  7.3 6.7 %collective-permute-start.1 = (f32[5,16,192]{2,1,0:T(8,128)S(1)}, f32[5,16,192]{2,1,0:T(8,128)S(1)}, u32[]{:S(2)}, u32[]{:S(2)}) collective-permute-start(f32[5,16,192]{2,1,0:T(8,128)S(1)} %get-tuple-element.11), channel_id=1, source_target_pairs={{1,0},{2,1},{3,2},{4,3},{5,4},{6,5},{7,6},{0,7},{9,8},{10,9},{11,1... | collective-permute-start | bytes 184328 | tf_op jit(solution)/shard_map/ppermute | solution.py:333
  14.1 17.2 %collective-permute-start.2 = (f32[5,8,768]{2,1,0:T(8,128)S(1)}, f32[5,8,768]{2,1,0:T(8,128)S(1)}, u32[]{:S(2)}, u32[]{:S(2)}) collective-permute-start(f32[5,8,768]{2,1,0:T(8,128)S(1)} %get-tuple-element.10), channel_id=1, source_target_pairs={{0,8},{8,16},{16,24},{24,32},{32,40},{40,48},{48,56},{56,64},{64,7... | collective-permute-start | bytes 368648 | tf_op jit(solution)/shard_map/ppermute | solution.py:337
  19.7 12.6 %collective-permute-start.3 = (f32[5,8,768]{2,1,0:T(8,128)S(1)}, f32[5,8,768]{2,1,0:T(8,128)S(1)}, u32[]{:S(2)}, u32[]{:S(2)}) collective-permute-start(f32[5,8,768]{2,1,0:T(8,128)S(1)} %get-tuple-element.9), channel_id=1, source_target_pairs={{8,0},{16,8},{24,16},{32,24},{40,32},{48,40},{56,48},{64,56},{72,6... | collective-permute-start | bytes 368648 | tf_op jit(solution)/shard_map/ppermute | solution.py:338

commit v3 on v2

--- a/solution.py
+++ b/solution.py
@@ -311,8 +311,10 @@
 ]
 
 
-def all_sum(part, axes, count):
-    return jnp.sum(lax.all_to_all(part, axes, 0, 0, tiled=True), axis=0)
+def all_sum(part, axes, count, first):
+    order = [[(i + first) % count for i in range(count)]]
+    parts = lax.all_to_all(part, axes, 0, 0, tiled=True, axis_index_groups=order)
+    return jnp.sum(parts, axis=0)
 
 
 def make_body(gz, gy, near, far, n_near, n_far, n_gz, n_gy):
@@ -357,8 +359,8 @@
             compiler_params=pltpu.CompilerParams(vmem_limit_bytes=40 * 1024 * 1024),
             name="lattice_window",
         )(zbase, left, own, right, top, bot)
-        line = all_sum(part, near, n_near)
-        line = all_sum(jnp.broadcast_to(line, (n_far, 128)), far, n_far)
+        line = all_sum(part, near, n_near, n_gy + 5 * n_gy // 8)
+        line = all_sum(jnp.broadcast_to(line, (n_far, 128)), far, n_far, 9 * n_far // 16)
         return temp, flow, line[0] * (2.0 / (NX * height))
 
     return body

time: 103 us -> 86.4 us (0.84)
  blocking collectives: 56.6 us -> 39.6 us
    all_to_all x2, blocking collectives: 56.6 us -> 39.6 us  [all_sum(): lax.all_to_all(part, axes, 0, 0, tiled=True, axis_index_groups=order)]
where the time goes in v3:
time: 86.4 us; the launch traced here: 85.5 us
  blocking collectives  39.6 us (46%)
  starting transfers between devices  26.9 us (31%)
  Pallas kernels  12.4 us (14%)
  waiting for transfers between devices  3.43 us (4%)
  between operations  1.88 us (2%)
  other arithmetic  1.08 us (1%)
    all_to_all x2, blocking collectives, all_sum(): lax.all_to_all(part, axes, 0, 0, tiled=True, axis_index_groups=order)  39.6 us
    pallas_call x1, Pallas kernels, body(): pl.pallas_call(window, in_specs=[pl.BlockSpec(memory_space=pltpu.SMEM)] +...  12.4 us
    ppermute x1, starting transfers between devices, body(): bot = lax.ppermute(wide[:, :HALO], gz, down)  11.6 us
    ppermute x1, starting transfers between devices, body(): left = lax.ppermute(own[:, :, cells - rim:], gy, up)  5.65 us
    ppermute x1, starting transfers between devices, body(): top = lax.ppermute(wide[:, slab - HALO:], gz, up)  5.54 us
    ppermute x1, starting transfers between devices, body(): right = lax.ppermute(own[:, :, :rim], gy, down)  4.12 us
    ppermute x1, waiting for transfers between devices, body(): right = lax.ppermute(own[:, :, :rim], gy, down)  2.56 us
  transfers between devices with their start and end apart: 4, of which 2 were waited for; matrix products, arithmetic and copies ran while one was open for 0% of the time, Pallas kernels for 0%

profile of v3, /device:TPU:1, one launch (start us, length us, event | category | flops | bytes accessed | tf_op | source)
XLA Modules:
  0.0 85.5 jit_solution(12334297147545236257)
XLA Ops:
  0.6 0.0 copy-start
  0.6 0.8 convert_bitcast_fusion
  1.4 0.1 copy-done
  1.5 0.1 fusion.1
  1.6 5.7 %collective-permute-start = (f32[5,16,192]{2,1,0:T(8,128)S(1)}, f32[5,16,192]{2,1,0:T(8,128)S(1)}, u32[]{:S(2)}, u32[]{:S(2)}) collective-permute-start(f32[5,16,192]{2,1,0:T(8,128)S(1)} %get-tuple-element.12), channel_id=1, source_target_pairs={{0,1},{1,2},{2,3},{3,4},{4,5},{5,6},{6,7},{7,0},{8,9},{9,10},{10,1... | collective-permute-start | bytes 184328 | tf_op jit(solution)/shard_map/ppermute | solution.py:334
  7.3 4.1 %collective-permute-start.1 = (f32[5,16,192]{2,1,0:T(8,128)S(1)}, f32[5,16,192]{2,1,0:T(8,128)S(1)}, u32[]{:S(2)}, u32[]{:S(2)}) collective-permute-start(f32[5,16,192]{2,1,0:T(8,128)S(1)} %get-tuple-element.11), channel_id=1, source_target_pairs={{1,0},{2,1},{3,2},{4,3},{5,4},{6,5},{7,6},{0,7},{9,8},{10,9},{11,1... | collective-permute-start | bytes 184328 | tf_op jit(solution)/shard_map/ppermute | solution.py:335
  11.4 0.0 collective-permute-done.left
  11.4 2.6 %collective-permute-done.1.right = f32[5,16,192]{2,1,0:T(8,128)S(1)} collective-permute-done((f32[5,16,192]{2,1,0:T(8,128)S(1)}, f32[5,16,192]{2,1,0:T(8,128)S(1)}, u32[]{:S(2)}, u32[]{:S(2)}) %collective-permute-start.1) | collective-permute-done | bytes 61472 | tf_op jit(solution)/shard_map/ppermute | solution.py:335
  14.0 0.1 pad_maximum_fusion
  14.1 5.5 %collective-permute-start.2 = (f32[5,8,768]{2,1,0:T(8,128)S(1)}, f32[5,8,768]{2,1,0:T(8,128)S(1)}, u32[]{:S(2)}, u32[]{:S(2)}) collective-permute-start(f32[5,8,768]{2,1,0:T(8,128)S(1)} %get-tuple-element.10), channel_id=1, source_target_pairs={{0,8},{8,16},{16,24},{24,32},{32,40},{40,48},{48,56},{56,64},{64,7... | collective-permute-start | bytes 368648 | tf_op jit(solution)/shard_map/ppermute | solution.py:339
  19.7 11.6 %collective-permute-start.3 = (f32[5,8,768]{2,1,0:T(8,128)S(1)}, f32[5,8,768]{2,1,0:T(8,128)S(1)}, u32[]{:S(2)}, u32[]{:S(2)}) collective-permute-start(f32[5,8,768]{2,1,0:T(8,128)S(1)} %get-tuple-element.9), channel_id=1, source_target_pairs={{8,0},{16,8},{24,16},{32,24},{40,32},{48,40},{56,48},{64,56},{72,6... | collective-permute-start | bytes 368648 | tf_op jit(solution)/shard_map/ppermute | solution.py:340
  31.3 0.1 pad_maximum_fusion.2.zbase
  31.4 0.0 collective-permute-done.2.top
  31.4 0.9 %collective-permute-done.3.bot = f32[5,8,768]{2,1,0:T(8,128)S(1)} collective-permute-done((f32[5,8,768]{2,1,0:T(8,128)S(1)}, f32[5,8,768]{2,1,0:T(8,128)S(1)}, u32[]{:S(2)}, u32[]{:S(2)}) %collective-permute-start.3) | collective-permute-done | bytes 122912 | tf_op jit(solution)/shard_map/ppermute | solution.py:340
  32.2 12.4 %lattice_window.1 = (f32[16,384]{1,0:T(8,128)}, f32[3,16,384]{2,1,0:T(8,128)}, f32[32,128]{1,0:T(8,128)S(1)}) custom-call(f32[2]{0:T(128)S(1)} %pad_maximum_fusion.2.zbase, f32[5,16,192]{2,1,0:T(8,128)S(1)} %collective-permute-done.left, f32[5,16,384]{2,1,0:T(8,128)S(1)} %pad_maximum_fusion.1.own, f32[5,16,192]{2,1,0:T(8,128)S(1)} %collective-permute-done.1.right, ...), custom_call_target="tpu_custom_call" | custom-call | tf_op jit(solution)/shard_map/lattice_window/pallas_call | solution.py:349
  44.6 15.3 %all_to_all.15 = f32[32,1,128]{2,1,0:T(1,128)S(1)} all-to-all(f32[32,1,128]{2,1,0:T(1,128)S(1)} %bitcast.11), channel_id=1, replica_groups={{13,14,15,512,513,514,515,516,517,518,519,520,521,522,523,524,525,526,5..., dimensions={0} | all-to-all | bytes 32768 | tf_op jit(solution)/shard_map/all_to_all | solution.py:316
  59.9 0.1 reduce_sum.18
  59.9 24.4 %all_to_all.16 = f32[32,1,128]{2,1,0:T(1,128)S(1)} all-to-all(f32[32,1,128]{2,1,0:T(1,128)S(1)} %broadcast_in_dim.11), channel_id=1, replica_groups={{288,304,320,336,352,368,384,400,416,432,448,464,480,496,0,16,32,48,64,..., dimensions={0} | all-to-all | bytes 32768 | tf_op jit(solution)/shard_map/all_to_all | solution.py:316
  (4 shorter events, 0.1 us)
Async XLA Ops:
  0.6 0.9 %copy-start = (f32[3,16,384]{2,1,0:T(8,128)S(1)}, f32[3,16,384]{2,1,0:T(8,128)}, u32[]{:S(2)}) copy-start(f32[3,16,384]{2,1,0:T(8,128)} %param.5) | copy-start | bytes 221188
  1.6 9.8 %collective-permute-start = (f32[5,16,192]{2,1,0:T(8,128)S(1)}, f32[5,16,192]{2,1,0:T(8,128)S(1)}, u32[]{:S(2)}, u32[]{:S(2)}) collective-permute-start(f32[5,16,192]{2,1,0:T(8,128)S(1)} %get-tuple-element.12), channel_id=1, source_target_pairs={{0,1},{1,2},{2,3},{3,4},{4,5},{5,6},{6,7},{7,0},{8,9},{9,10},{10,1... | collective-permute-start | bytes 184328 | tf_op jit(solution)/shard_map/ppermute | solution.py:334
  7.3 6.7 %collective-permute-start.1 = (f32[5,16,192]{2,1,0:T(8,128)S(1)}, f32[5,16,192]{2,1,0:T(8,128)S(1)}, u32[]{:S(2)}, u32[]{:S(2)}) collective-permute-start(f32[5,16,192]{2,1,0:T(8,128)S(1)} %get-tuple-element.11), channel_id=1, source_target_pairs={{1,0},{2,1},{3,2},{4,3},{5,4},{6,5},{7,6},{0,7},{9,8},{10,9},{11,1... | collective-permute-start | bytes 184328 | tf_op jit(solution)/shard_map/ppermute | solution.py:335
  14.1 17.2 %collective-permute-start.2 = (f32[5,8,768]{2,1,0:T(8,128)S(1)}, f32[5,8,768]{2,1,0:T(8,128)S(1)}, u32[]{:S(2)}, u32[]{:S(2)}) collective-permute-start(f32[5,8,768]{2,1,0:T(8,128)S(1)} %get-tuple-element.10), channel_id=1, source_target_pairs={{0,8},{8,16},{16,24},{24,32},{32,40},{40,48},{48,56},{56,64},{64,7... | collective-permute-start | bytes 368648 | tf_op jit(solution)/shard_map/ppermute | solution.py:339
  19.7 12.6 %collective-permute-start.3 = (f32[5,8,768]{2,1,0:T(8,128)S(1)}, f32[5,8,768]{2,1,0:T(8,128)S(1)}, u32[]{:S(2)}, u32[]{:S(2)}) collective-permute-start(f32[5,8,768]{2,1,0:T(8,128)S(1)} %get-tuple-element.9), channel_id=1, source_target_pairs={{8,0},{16,8},{24,16},{32,24},{40,32},{48,40},{56,48},{64,56},{72,6... | collective-permute-start | bytes 368648 | tf_op jit(solution)/shard_map/ppermute | solution.py:340

commit v4 on v3

--- a/solution.py
+++ b/solution.py
@@ -188,22 +188,34 @@
         f.append(jnp.where(open_, moved, tile(src, OPP[i], s, xt)))
         if i < 7:
             back = tile(src, 19 + OPP[i], s, xt)
-            coeff = pl.ds(8 * xt, 8)
-            back = wa[i - 1, s, coeff, :] * back + wb[i - 1, s, coeff, :]
+            c = LAT19[i]
+            near = (c[2] % 3, s + 1 - c[1], pl.ds(8 + 8 * xt - c[0], 8))
+            back = wa[near] * back + wb[near]
             g.append(jnp.where(open_, moved_tile(src, 19 + i, s, xt), back))
     return f, g
 
 
 def window(zbase, left, own, right, top, bot, temp_out, flow_out, part_out,
-           stage, inp, kinds, pops, wa, wb, res):
+           stage, inp, pops, wa, wb, res):
     height = zbase[1]
     for a in range(5):
-        blocks = (left[a], own[a, :, 0:192], own[a, :, 192:384], right[a])
-        for q in range(4):
-            r0 = 32 * q
-            stage[a, r0 : r0 + 8, 0:192] = top[a, :, 192 * q : 192 * q + 192]
-            stage[a, r0 + 8 : r0 + 24, 0:192] = blocks[q]
-            stage[a, r0 + 24 : r0 + 32, 0:192] = bot[a, :, 192 * q : 192 * q + 192]
+        p, half = 5 + a // 2, 64 * (a % 2)
+        parts = (
+            (8, 16, [own[3 * a + j] for j in range(3)], left, right),
+            (0, 8, [top[3 * a + j] for j in range(3)], top.at[15:23], top.at[23:31]),
+            (24, 8, [bot[3 * a + j] for j in range(3)], bot.at[15:23], bot.at[23:31]),
+        )
+        for z0, n, mid, lo, hi in parts:
+            low = ((0, lo[a]), (3, hi[a]), (1, mid[0]), (2, mid[2]))
+            ends = (lo[p, :, half : half + 64], hi[p, :, half : half + 64])
+            for q, v in low:
+                r = slice(32 * q + z0, 32 * q + z0 + n)
+                if q % 2:
+                    stage[a, r, 0:128] = v
+                    stage[a, r, 128:192] = ends[1] if q == 3 else mid[1][:, 0:64]
+                else:
+                    stage[a, r, 0:64] = mid[1][:, 64:128] if q else ends[0]
+                    stage[a, r, 64:192] = v
         inp[a, 0:16] = stage[a, :, 0:128].T.reshape(16, 8, 128)
         inp[a, 16:24] = stage[a, :, 128:256].T[0:64].reshape(8, 8, 128)
 
@@ -213,12 +225,19 @@
     zpos = zbase[0] + zin.astype(jnp.float32)
     ramp = 0.5 - 0.75 * (zpos + 0.5) / height
 
-    def first(s, carry):
+    def first(s):
         for xt in range(XT):
             kind = inp[0, s * XT + xt]
-            put(kinds, 0, s + 1, xt, kind)
-            put(kinds, 1, s + 1, xt, shift_lanes(kind, 1))
-            put(kinds, 2, s + 1, xt, shift_lanes(kind, -1))
+            hot, cold = kind == 2.0, kind == 3.0
+            sign = jnp.where(hot | cold, -1.0, 1.0)
+            gain = jnp.where(hot, 0.125, jnp.where(cold, -0.125, 0.0))
+            for ref, v in ((wa, sign), (wb, gain)):
+                for chan in range(3):
+                    put(ref, chan, s + 1, xt, shift_lanes(v, (0, 1, -1)[chan]) if chan else v)
+                if s == 0:
+                    put(ref, 0, NS + 1, xt, shift_lanes(v, -32))
+                if s == NS - 1:
+                    put(ref, 0, 0, xt, shift_lanes(v, 32))
             fluid = kind == 0.0
             u = [inp[2 + a, s * XT + xt] for a in range(3)]
             temp = ramp + 0.05 * inp[1, s * XT + xt]
@@ -231,26 +250,10 @@
                 f.append(eq + ua)
                 f.append(eq - ua)
             put_all(pops.at[0], s, xt, f)
-        return carry
-
-    lax.fori_loop(0, NS, first, 0, unroll=True)
+
+    for s in range(NS):
+        first(s)
     copies(pops.at[0])
-    for xt in range(XT):
-        put(kinds, 0, NS + 1, xt, shift_lanes(tile(kinds, 0, 0, xt), -32))
-        put(kinds, 0, 0, xt, shift_lanes(tile(kinds, 0, NS - 1, xt), 32))
-
-    def walls_of(s, carry):
-        for xt in range(XT):
-            rows = pl.ds(8 * xt, 8)
-            for i in range(1, 7):
-                c = LAT19[i]
-                near = kinds[(0, 1, 2)[c[2]], s + 1 - c[1], pl.ds(8 + 8 * xt - c[0], 8), :]
-                hot, cold = near == 2.0, near == 3.0
-                wa[i - 1, s, rows, :] = jnp.where(hot | cold, -1.0, 1.0)
-                wb[i - 1, s, rows, :] = jnp.where(hot, 0.125, jnp.where(cold, -0.125, 0.0))
-        return carry
-
-    lax.fori_loop(0, NS, walls_of, 0, unroll=True)
 
     def step(k, carry):
         src, dst = pops.at[lax.rem(k + 1, 2)], pops.at[lax.rem(k, 2)]
@@ -274,14 +277,14 @@
             rho, mx, my, mz = moments(f)
             fluid = f[0] < BIG
             inv = inverse(rho)
-            kind = tile(kinds, 0, s, xt)
+            kind = inp[0, s * XT + xt]
             walls = jnp.where(kind == 2.0, 0.5, jnp.where(kind == 3.0, -0.5, 0.0))
             temp = g[0] + (g[1] + g[2]) + (g[3] + g[4]) + (g[5] + g[6])
             temp = jnp.where(fluid, temp, walls)
             res[0, s * XT + xt] = temp
             for a, m in enumerate((mx, my, mz)):
                 res[1 + a, s * XT + xt] = jnp.where(fluid, m * inv, 0.0)
-            heated = fluid & mine & (kinds[0, s, pl.ds(8 + 8 * xt, 8), :] == 2.0)
+            heated = fluid & mine & (wb[0, s, pl.ds(8 + 8 * xt, 8), :] == 0.125)
             total = total + jnp.where(heated, 0.5 - temp, 0.0)
         return total
 
@@ -303,12 +306,41 @@
 SCRATCH = [
     pltpu.VMEM((5, 128, 256), jnp.float32),
     pltpu.VMEM((5, NS * XT, 8, 128), jnp.float32),
+    pltpu.VMEM((2, NCHAN, NS + 2, ROWS, 128), jnp.float32),
     pltpu.VMEM((3, NS + 2, ROWS, 128), jnp.float32),
-    pltpu.VMEM((2, NCHAN, NS + 2, ROWS, 128), jnp.float32),
-    pltpu.VMEM((6, NS, NX, 128), jnp.float32),
-    pltpu.VMEM((6, NS, NX, 128), jnp.float32),
+    pltpu.VMEM((3, NS + 2, ROWS, 128), jnp.float32),
     pltpu.VMEM((4, 32, 8, 128), jnp.float32),
 ]
+
+
+def pack_sides(cell_type, perturb, velocity, own, low, high, kind, noise, speed, sems):
+    moves = [
+        pltpu.make_async_copy(src, dst, sems.at[i])
+        for i, (src, dst) in enumerate(((cell_type, kind), (perturb, noise), (velocity, speed)))
+    ]
+    for move in moves:
+        move.start()
+    for move in moves:
+        move.wait()
+    fields = [kind[...].astype(jnp.float32), noise[...].astype(jnp.float32)]
+    fields += [speed[a] for a in range(3)]
+    for a, f in enumerate(fields):
+        for j in range(3):
+            own[3 * a + j] = f[:, 128 * j : 128 * j + 128]
+        low[a] = f[:, 0:128]
+        high[a] = f[:, 256:384]
+    for p in range(3):
+        one, two = fields[2 * p], fields[min(2 * p + 1, 4)]
+        low[5 + p] = jnp.concatenate([one[:, 128:192], two[:, 128:192]], axis=1)
+        high[5 + p] = jnp.concatenate([one[:, 192:256], two[:, 192:256]], axis=1)
+
+
+def pack_ends(own, left, right, first, final):
+    rows = own.shape[1]
+    for ref, at in ((own, 0), (left, 15), (right, 23)):
+        n = ref.shape[0]
+        first[at : at + n] = ref[:, 0:HALO]
+        final[at : at + n] = ref[:, rows - HALO : rows]
 
 
 def all_sum(part, axes, count, first):
@@ -321,31 +353,46 @@
     def body(cell_type, perturb, velocity):
         slab, cells = cell_type.shape
         height = slab * n_gz
-        own = jnp.concatenate(
-            [
-                cell_type.astype(jnp.float32)[None],
-                perturb.astype(jnp.float32)[None],
-                velocity,
-            ]
-        )
-        rim = HALO * NX
+        vmem = pl.BlockSpec(memory_space=pltpu.VMEM)
+        f32 = jnp.float32
+
+        def tiles(n, rows):
+            return jax.ShapeDtypeStruct((n, rows, 128), f32)
+
+        own, low, high = pl.pallas_call(
+            pack_sides,
+            in_specs=[pl.BlockSpec(memory_space=pl.ANY)] * 3,
+            out_specs=[vmem] * 3,
+            out_shape=[tiles(15, slab), tiles(8, slab), tiles(8, slab)],
+            scratch_shapes=[
+                pltpu.VMEM((slab, cells), jnp.int32),
+                pltpu.VMEM((slab, cells), jnp.int32),
+                pltpu.VMEM((3, slab, cells), f32),
+                pltpu.SemaphoreType.DMA((3,)),
+            ],
+            name="pack_sides",
+        )(cell_type, perturb, velocity)
         up = [(i, (i + 1) % n_gy) for i in range(n_gy)]
         down = [((i + 1) % n_gy, i) for i in range(n_gy)]
-        left = lax.ppermute(own[:, :, cells - rim :], gy, up)
-        right = lax.ppermute(own[:, :, :rim], gy, down)
-        wide = jnp.concatenate([left, own, right], axis=2)
+        left = lax.ppermute(high, gy, up)
+        right = lax.ppermute(low, gy, down)
+        first, final = pl.pallas_call(
+            pack_ends,
+            in_specs=[vmem] * 3,
+            out_specs=[vmem] * 2,
+            out_shape=[tiles(31, HALO), tiles(31, HALO)],
+            name="pack_ends",
+        )(own, left, right)
         up = [(i, (i + 1) % n_gz) for i in range(n_gz)]
         down = [((i + 1) % n_gz, i) for i in range(n_gz)]
-        top = lax.ppermute(wide[:, slab - HALO :], gz, up)
-        bot = lax.ppermute(wide[:, :HALO], gz, down)
+        top = lax.ppermute(final, gz, up)
+        bot = lax.ppermute(first, gz, down)
         zbase = jnp.stack(
             [
                 (lax.axis_index(gz) * slab - HALO).astype(jnp.float32),
                 jnp.float32(height),
             ]
         )
-        vmem = pl.BlockSpec(memory_space=pltpu.VMEM)
-        f32 = jnp.float32
         temp, flow, part = pl.pallas_call(
             window,
             in_specs=[pl.BlockSpec(memory_space=pltpu.SMEM)] + [vmem] * 5,

time: 86.4 us -> 91.1 us (1.054)
  Pallas kernels: 12.4 us -> 15.5 us
  local copies, waits for them, and re-layouts: 0.2 us -> 2.33 us
  other arithmetic: 1.08 us -> 0.14 us
    pallas_call x0 -> x2, Pallas kernels: none -> 3.34 us  [the longest x1 1.69 us: body(): pl.pallas_call(pack_ends, in_specs=[vmem] * 3, out_specs=[vmem] * 2, out_...]
    unnamed x2 -> x10, local copies, waits for them, and re-layouts: 0.09 us -> 2.31 us
where the time goes in v4:
time: 91.1 us; the launch traced here: 90.1 us
  blocking collectives  39.5 us (43%)
  starting transfers between devices  27 us (30%)
  Pallas kernels  15.5 us (17%)
  waiting for transfers between devices  3.67 us (4%)
  local copies, waits for them, and re-layouts  2.33 us (3%)
  between operations  1.88 us (2%)
    all_to_all x2, blocking collectives, all_sum(): lax.all_to_all(part, axes, 0, 0, tiled=True, axis_index_groups=order)  39.5 us
    pallas_call x1, Pallas kernels, body(): pl.pallas_call(window, in_specs=[pl.BlockSpec(memory_space=pltpu.SMEM)] +...  12.2 us
    ppermute x1, starting transfers between devices, body(): bot = lax.ppermute(first, gz, down)  11.7 us
    ppermute x1, starting transfers between devices, body(): left = lax.ppermute(high, gy, up)  5.65 us
    ppermute x1, starting transfers between devices, body(): top = lax.ppermute(final, gz, up)  5.52 us
    ppermute x1, starting transfers between devices, body(): right = lax.ppermute(low, gy, down)  4.11 us
    ppermute x1, waiting for transfers between devices, body(): right = lax.ppermute(low, gy, down)  2.58 us
    unnamed x10, local copies, waits for them, and re-layouts  2.31 us
  transfers between devices with their start and end apart: 4, of which 2 were waited for; matrix products, arithmetic and copies ran while one was open for 0% of the time, Pallas kernels for 0%

profile of v4, /device:TPU:1, one launch (start us, length us, event | category | flops | bytes accessed | tf_op | source)
XLA Modules:
  0.0 90.1 jit_solution(8494251453983057259)
XLA Ops:
  0.6 1.7 %pack_sides.1 = (f32[15,16,128]{2,1,0:T(8,128)}, f32[8,16,128]{2,1,0:T(8,128)}, f32[8,16,128]{2,1,0:T(8,128)}) custom-call(s32[16,384]{1,0:T(8,128)} %cell_type.1, s32[16,384]{1,0:T(8,128)} %perturb.1, f32[3,16,384]{2,1,0:T(8,128)} %velocity.1), custom_call_target="tpu_custom_call" | custom-call | tf_op jit(solution)/shard_map/pack_sides/pallas_call | solution.py:362
  2.3 5.7 %collective-permute-start = (f32[8,16,128]{2,1,0:T(8,128)}, f32[8,16,128]{2,1,0:T(8,128)S(1)}, u32[]{:S(2)}, u32[]{:S(2)}) collective-permute-start(f32[8,16,128]{2,1,0:T(8,128)} %get-tuple-element.11), channel_id=1, source_target_pairs={{0,1},{1,2},{2,3},{3,4},{4,5},{5,6},{6,7},{7,0},{8,9},{9,10},{10,1... | collective-permute-start | bytes 196616 | tf_op jit(solution)/shard_map/ppermute | solution.py:377
  8.0 4.1 %collective-permute-start.1 = (f32[8,16,128]{2,1,0:T(8,128)}, f32[8,16,128]{2,1,0:T(8,128)S(1)}, u32[]{:S(2)}, u32[]{:S(2)}) collective-permute-start(f32[8,16,128]{2,1,0:T(8,128)} %get-tuple-element.13), channel_id=1, source_target_pairs={{1,0},{2,1},{3,2},{4,3},{5,4},{6,5},{7,6},{0,7},{9,8},{10,9},{11,1... | collective-permute-start | bytes 196616 | tf_op jit(solution)/shard_map/ppermute | solution.py:378
  12.1 0.0 collective-permute-done.left
  12.1 0.0 copy-start.1
  12.1 2.6 %collective-permute-done.1.right = f32[8,16,128]{2,1,0:T(8,128)S(1)} collective-permute-done((f32[8,16,128]{2,1,0:T(8,128)}, f32[8,16,128]{2,1,0:T(8,128)S(1)}, u32[]{:S(2)}, u32[]{:S(2)}) %collective-permute-start.1) | collective-permute-done | bytes 65568 | tf_op jit(solution)/shard_map/ppermute | solution.py:378
  14.7 0.0 copy-start.3
  14.7 0.0 copy-done.1
  14.7 0.6 copy-done.3
  15.3 0.0 copy-start
  15.3 1.7 %pack_ends.1 = (f32[31,8,128]{2,1,0:T(8,128)}, f32[31,8,128]{2,1,0:T(8,128)}) custom-call(f32[15,16,128]{2,1,0:T(8,128)} %get-tuple-element.12.own, f32[8,16,128]{2,1,0:T(8,128)} %copy-done.1, f32[8,16,128]{2,1,0:T(8,128)} %copy-done.3), custom_call_target="tpu_custom_call" | custom-call | tf_op jit(solution)/shard_map/pack_ends/pallas_call | solution.py:379
  17.0 5.5 %collective-permute-start.2 = (f32[31,8,128]{2,1,0:T(8,128)}, f32[31,8,128]{2,1,0:T(8,128)S(1)}, u32[]{:S(2)}, u32[]{:S(2)}) collective-permute-start(f32[31,8,128]{2,1,0:T(8,128)} %get-tuple-element.14), channel_id=1, source_target_pairs={{0,8},{8,16},{16,24},{24,32},{32,40},{40,48},{48,56},{56,64},{64,7... | collective-permute-start | bytes 380936 | tf_op jit(solution)/shard_map/ppermute | solution.py:388
  22.5 11.7 %collective-permute-start.3 = (f32[31,8,128]{2,1,0:T(8,128)}, f32[31,8,128]{2,1,0:T(8,128)S(1)}, u32[]{:S(2)}, u32[]{:S(2)}) collective-permute-start(f32[31,8,128]{2,1,0:T(8,128)} %get-tuple-element.15), channel_id=1, source_target_pairs={{8,0},{16,8},{24,16},{32,24},{40,32},{48,40},{56,48},{64,56},{72,6... | collective-permute-start | bytes 380936 | tf_op jit(solution)/shard_map/ppermute | solution.py:389
  34.3 0.1 pad_maximum_fusion.zbase
  34.4 0.0 collective-permute-done.2.top
  34.4 1.1 %collective-permute-done.3.bot = f32[31,8,128]{2,1,0:T(8,128)S(1)} collective-permute-done((f32[31,8,128]{2,1,0:T(8,128)}, f32[31,8,128]{2,1,0:T(8,128)S(1)}, u32[]{:S(2)}, u32[]{:S(2)}) %collective-permute-start.3) | collective-permute-done | bytes 127008 | tf_op jit(solution)/shard_map/ppermute | solution.py:389
  35.4 0.0 copy-done
  35.4 0.0 copy-start.2
  35.4 0.8 copy-done.2
  36.3 0.0 copy-start.4
  36.3 0.8 copy-done.4
  37.1 12.2 %lattice_window.1 = (f32[16,384]{1,0:T(8,128)}, f32[3,16,384]{2,1,0:T(8,128)}, f32[32,128]{1,0:T(8,128)S(1)}) custom-call(f32[2]{0:T(128)S(1)} %pad_maximum_fusion.zbase, f32[8,16,128]{2,1,0:T(8,128)S(1)} %copy-done.2, f32[15,16,128]{2,1,0:T(8,128)S(1)} %copy-done, f32[8,16,128]{2,1,0:T(8,128)S(1)} %copy-done.4, ...), custom_call_target="tpu_custom_call" | custom-call | tf_op jit(solution)/shard_map/lattice_window/pallas_call | solution.py:396
  49.3 15.3 %all_to_all.15 = f32[32,1,128]{2,1,0:T(1,128)S(1)} all-to-all(f32[32,1,128]{2,1,0:T(1,128)S(1)} %bitcast.7), channel_id=1, replica_groups={{13,14,15,512,513,514,515,516,517,518,519,520,521,522,523,524,525,526,5..., dimensions={0} | all-to-all | bytes 32768 | tf_op jit(solution)/shard_map/all_to_all | solution.py:348
  64.6 0.1 reduce_sum.18
  64.6 24.3 %all_to_all.16 = f32[32,1,128]{2,1,0:T(1,128)S(1)} all-to-all(f32[32,1,128]{2,1,0:T(1,128)S(1)} %broadcast_in_dim.3), channel_id=1, replica_groups={{288,304,320,336,352,368,384,400,416,432,448,464,480,496,0,16,32,48,64,..., dimensions={0} | all-to-all | bytes 32768 | tf_op jit(solution)/shard_map/all_to_all | solution.py:348
  (2 shorter events, 0.0 us)
Async XLA Ops:
  2.3 9.8 %collective-permute-start = (f32[8,16,128]{2,1,0:T(8,128)}, f32[8,16,128]{2,1,0:T(8,128)S(1)}, u32[]{:S(2)}, u32[]{:S(2)}) collective-permute-start(f32[8,16,128]{2,1,0:T(8,128)} %get-tuple-element.11), channel_id=1, source_target_pairs={{0,1},{1,2},{2,3},{3,4},{4,5},{5,6},{6,7},{7,0},{8,9},{9,10},{10,1... | collective-permute-start | bytes 196616 | tf_op jit(solution)/shard_map/ppermute | solution.py:377
  8.0 6.7 %collective-permute-start.1 = (f32[8,16,128]{2,1,0:T(8,128)}, f32[8,16,128]{2,1,0:T(8,128)S(1)}, u32[]{:S(2)}, u32[]{:S(2)}) collective-permute-start(f32[8,16,128]{2,1,0:T(8,128)} %get-tuple-element.13), channel_id=1, source_target_pairs={{1,0},{2,1},{3,2},{4,3},{5,4},{6,5},{7,6},{0,7},{9,8},{10,9},{11,1... | collective-permute-start | bytes 196616 | tf_op jit(solution)/shard_map/ppermute | solution.py:378
  12.1 2.6 %copy-start.1 = (f32[8,16,128]{2,1,0:T(8,128)}, f32[8,16,128]{2,1,0:T(8,128)S(1)}, u32[]{:S(2)}) copy-start(f32[8,16,128]{2,1,0:T(8,128)S(1)} %collective-permute-done.left) | copy-start | bytes 196612
  14.7 0.6 copy-start.3
  15.3 20.1 %copy-start = (f32[15,16,128]{2,1,0:T(8,128)S(1)}, f32[15,16,128]{2,1,0:T(8,128)}, u32[]{:S(2)}) copy-start(f32[15,16,128]{2,1,0:T(8,128)} %get-tuple-element.12.own) | copy-start | bytes 368644
  17.0 17.4 %collective-permute-start.2 = (f32[31,8,128]{2,1,0:T(8,128)}, f32[31,8,128]{2,1,0:T(8,128)S(1)}, u32[]{:S(2)}, u32[]{:S(2)}) collective-permute-start(f32[31,8,128]{2,1,0:T(8,128)} %get-tuple-element.14), channel_id=1, source_target_pairs={{0,8},{8,16},{16,24},{24,32},{32,40},{40,48},{48,56},{56,64},{64,7... | collective-permute-start | bytes 380936 | tf_op jit(solution)/shard_map/ppermute | solution.py:388
  22.5 12.9 %collective-permute-start.3 = (f32[31,8,128]{2,1,0:T(8,128)}, f32[31,8,128]{2,1,0:T(8,128)S(1)}, u32[]{:S(2)}, u32[]{:S(2)}) collective-permute-start(f32[31,8,128]{2,1,0:T(8,128)} %get-tuple-element.15), channel_id=1, source_target_pairs={{8,0},{16,8},{24,16},{32,24},{40,32},{48,40},{56,48},{64,56},{72,6... | collective-permute-start | bytes 380936 | tf_op jit(solution)/shard_map/ppermute | solution.py:389
  35.4 0.8 copy-start.2
  36.3 0.8 copy-start.4

commit v5 on v3

--- a/solution.py
+++ b/solution.py
@@ -188,22 +188,30 @@
         f.append(jnp.where(open_, moved, tile(src, OPP[i], s, xt)))
         if i < 7:
             back = tile(src, 19 + OPP[i], s, xt)
-            coeff = pl.ds(8 * xt, 8)
-            back = wa[i - 1, s, coeff, :] * back + wb[i - 1, s, coeff, :]
+            c = LAT19[i]
+            near = (c[2] % 3, s + 1 - c[1], pl.ds(8 + 8 * xt - c[0], 8))
+            back = wa[near] * back + wb[near]
             g.append(jnp.where(open_, moved_tile(src, 19 + i, s, xt), back))
     return f, g
 
 
-def window(zbase, left, own, right, top, bot, temp_out, flow_out, part_out,
-           stage, inp, kinds, pops, wa, wb, res):
+def window(zbase, side_one, own, side_two, end_one, end_two, temp_out, flow_out, part_out,
+           stage, inp, pops, wa, wb, res):
     height = zbase[1]
+    even_y, even_z = zbase[2] > 0.5, zbase[3] > 0.5
+
+    def low_high(even, one, two):
+        return jnp.where(even, two, one), jnp.where(even, one, two)
+
     for a in range(5):
-        blocks = (left[a], own[a, :, 0:192], own[a, :, 192:384], right[a])
+        left, right = low_high(even_y, side_one[a], side_two[a])
+        top, bot = low_high(even_z, end_one[a], end_two[a])
+        blocks = (left, own[a, :, 0:192], own[a, :, 192:384], right)
         for q in range(4):
             r0 = 32 * q
-            stage[a, r0 : r0 + 8, 0:192] = top[a, :, 192 * q : 192 * q + 192]
+            stage[a, r0 : r0 + 8, 0:192] = top[:, 192 * q : 192 * q + 192]
             stage[a, r0 + 8 : r0 + 24, 0:192] = blocks[q]
-            stage[a, r0 + 24 : r0 + 32, 0:192] = bot[a, :, 192 * q : 192 * q + 192]
+            stage[a, r0 + 24 : r0 + 32, 0:192] = bot[:, 192 * q : 192 * q + 192]
         inp[a, 0:16] = stage[a, :, 0:128].T.reshape(16, 8, 128)
         inp[a, 16:24] = stage[a, :, 128:256].T[0:64].reshape(8, 8, 128)
 
@@ -213,12 +221,19 @@
     zpos = zbase[0] + zin.astype(jnp.float32)
     ramp = 0.5 - 0.75 * (zpos + 0.5) / height
 
-    def first(s, carry):
+    def first(s):
         for xt in range(XT):
             kind = inp[0, s * XT + xt]
-            put(kinds, 0, s + 1, xt, kind)
-            put(kinds, 1, s + 1, xt, shift_lanes(kind, 1))
-            put(kinds, 2, s + 1, xt, shift_lanes(kind, -1))
+            hot, cold = kind == 2.0, kind == 3.0
+            sign = jnp.where(hot | cold, -1.0, 1.0)
+            gain = jnp.where(hot, 0.125, jnp.where(cold, -0.125, 0.0))
+            for ref, v in ((wa, sign), (wb, gain)):
+                for chan in range(3):
+                    put(ref, chan, s + 1, xt, shift_lanes(v, (0, 1, -1)[chan]) if chan else v)
+                if s == 0:
+                    put(ref, 0, NS + 1, xt, shift_lanes(v, -32))
+                if s == NS - 1:
+                    put(ref, 0, 0, xt, shift_lanes(v, 32))
             fluid = kind == 0.0
             u = [inp[2 + a, s * XT + xt] for a in range(3)]
             temp = ramp + 0.05 * inp[1, s * XT + xt]
@@ -231,26 +246,10 @@
                 f.append(eq + ua)
                 f.append(eq - ua)
             put_all(pops.at[0], s, xt, f)
-        return carry
-
-    lax.fori_loop(0, NS, first, 0, unroll=True)
+
+    for s in range(NS):
+        first(s)
     copies(pops.at[0])
-    for xt in range(XT):
-        put(kinds, 0, NS + 1, xt, shift_lanes(tile(kinds, 0, 0, xt), -32))
-        put(kinds, 0, 0, xt, shift_lanes(tile(kinds, 0, NS - 1, xt), 32))
-
-    def walls_of(s, carry):
-        for xt in range(XT):
-            rows = pl.ds(8 * xt, 8)
-            for i in range(1, 7):
-                c = LAT19[i]
-                near = kinds[(0, 1, 2)[c[2]], s + 1 - c[1], pl.ds(8 + 8 * xt - c[0], 8), :]
-                hot, cold = near == 2.0, near == 3.0
-                wa[i - 1, s, rows, :] = jnp.where(hot | cold, -1.0, 1.0)
-                wb[i - 1, s, rows, :] = jnp.where(hot, 0.125, jnp.where(cold, -0.125, 0.0))
-        return carry
-
-    lax.fori_loop(0, NS, walls_of, 0, unroll=True)
 
     def step(k, carry):
         src, dst = pops.at[lax.rem(k + 1, 2)], pops.at[lax.rem(k, 2)]
@@ -274,14 +273,14 @@
             rho, mx, my, mz = moments(f)
             fluid = f[0] < BIG
             inv = inverse(rho)
-            kind = tile(kinds, 0, s, xt)
+            kind = inp[0, s * XT + xt]
             walls = jnp.where(kind == 2.0, 0.5, jnp.where(kind == 3.0, -0.5, 0.0))
             temp = g[0] + (g[1] + g[2]) + (g[3] + g[4]) + (g[5] + g[6])
             temp = jnp.where(fluid, temp, walls)
             res[0, s * XT + xt] = temp
             for a, m in enumerate((mx, my, mz)):
                 res[1 + a, s * XT + xt] = jnp.where(fluid, m * inv, 0.0)
-            heated = fluid & mine & (kinds[0, s, pl.ds(8 + 8 * xt, 8), :] == 2.0)
+            heated = fluid & mine & (wb[0, s, pl.ds(8 + 8 * xt, 8), :] == 0.125)
             total = total + jnp.where(heated, 0.5 - temp, 0.0)
         return total
 
@@ -303,10 +302,9 @@
 SCRATCH = [
     pltpu.VMEM((5, 128, 256), jnp.float32),
     pltpu.VMEM((5, NS * XT, 8, 128), jnp.float32),
+    pltpu.VMEM((2, NCHAN, NS + 2, ROWS, 128), jnp.float32),
     pltpu.VMEM((3, NS + 2, ROWS, 128), jnp.float32),
-    pltpu.VMEM((2, NCHAN, NS + 2, ROWS, 128), jnp.float32),
-    pltpu.VMEM((6, NS, NX, 128), jnp.float32),
-    pltpu.VMEM((6, NS, NX, 128), jnp.float32),
+    pltpu.VMEM((3, NS + 2, ROWS, 128), jnp.float32),
     pltpu.VMEM((4, 32, 8, 128), jnp.float32),
 ]
 
@@ -315,6 +313,15 @@
     order = [[(i + first) % count for i in range(count)]]
     parts = lax.all_to_all(part, axes, 0, 0, tiled=True, axis_index_groups=order)
     return jnp.sum(parts, axis=0)
+
+
+def swap(axis, count, even, head, tail):
+    near = [(i, i ^ 1) for i in range(count)]
+    far = [(i, (((i + 1) % count) ^ 1) - 1) for i in range(count)]
+    far = [(i, j % count) for i, j in far]
+    two = lax.ppermute(jnp.where(even, head, tail), axis, far)
+    one = lax.ppermute(jnp.where(even, tail, head), axis, near)
+    return one, two
 
 
 def make_body(gz, gy, near, far, n_near, n_far, n_gz, n_gy):
@@ -329,19 +336,19 @@
             ]
         )
         rim = HALO * NX
-        up = [(i, (i + 1) % n_gy) for i in range(n_gy)]
-        down = [((i + 1) % n_gy, i) for i in range(n_gy)]
-        left = lax.ppermute(own[:, :, cells - rim :], gy, up)
-        right = lax.ppermute(own[:, :, :rim], gy, down)
+        even_y = (lax.axis_index(gy) & 1) == 0
+        even_z = (lax.axis_index(gz[-1]) & 1) == 0
+        sides = swap(gy, n_gy, even_y, own[:, :, :rim], own[:, :, cells - rim :])
+        left = jnp.where(even_y, sides[1], sides[0])
+        right = jnp.where(even_y, sides[0], sides[1])
         wide = jnp.concatenate([left, own, right], axis=2)
-        up = [(i, (i + 1) % n_gz) for i in range(n_gz)]
-        down = [((i + 1) % n_gz, i) for i in range(n_gz)]
-        top = lax.ppermute(wide[:, slab - HALO :], gz, up)
-        bot = lax.ppermute(wide[:, :HALO], gz, down)
+        ends = swap(gz, n_gz, even_z, wide[:, :HALO], wide[:, slab - HALO :])
         zbase = jnp.stack(
             [
                 (lax.axis_index(gz) * slab - HALO).astype(jnp.float32),
                 jnp.float32(height),
+                even_y.astype(jnp.float32),
+                even_z.astype(jnp.float32),
             ]
         )
         vmem = pl.BlockSpec(memory_space=pltpu.VMEM)
@@ -358,7 +365,7 @@
             scratch_shapes=SCRATCH,
             compiler_params=pltpu.CompilerParams(vmem_limit_bytes=40 * 1024 * 1024),
             name="lattice_window",
-        )(zbase, left, own, right, top, bot)
+        )(zbase, sides[0], own, sides[1], ends[0], ends[1])
         line = all_sum(part, near, n_near, n_gy + 5 * n_gy // 8)
         line = all_sum(jnp.broadcast_to(line, (n_far, 128)), far, n_far, 9 * n_far // 16)
         return temp, flow, line[0] * (2.0 / (NX * height))

time: 86.4 us -> 84.6 us (0.979)
  blocking collectives: 39.6 us -> 32.2 us
  starting transfers between devices: 26.9 us -> 30.6 us
  waiting for transfers between devices: 3.43 us -> 5.6 us
    all_to_all x2, blocking collectives: 39.6 us -> 32.2 us  [all_sum(): lax.all_to_all(part, axes, 0, 0, tiled=True, axis_index_groups=order)]
    ppermute x4, starting transfers between devices: 26.9 us -> 30.6 us  [the longest x2 17.2 us: swap(): one = lax.ppermute(jnp.where(even, tail, head), axis, near)]
    ppermute x4, waiting for transfers between devices: 3.43 us -> 5.6 us  [the longest x2 5.6 us: swap(): one = lax.ppermute(jnp.where(even, tail, head), axis, near)]
where the time goes in v5:
time: 84.6 us; the launch traced here: 83.7 us
  blocking collectives  32.2 us (38%)
  starting transfers between devices  30.6 us (36%)
  Pallas kernels  12.1 us (14%)
  waiting for transfers between devices  5.6 us (7%)
  between operations  1.92 us (2%)
  other arithmetic  1.2 us (1%)
    all_to_all x2, blocking collectives, all_sum(): lax.all_to_all(part, axes, 0, 0, tiled=True, axis_index_groups=order)  32.2 us
    ppermute x2, starting transfers between devices, swap(): one = lax.ppermute(jnp.where(even, tail, head), axis, near)  17.2 us
    ppermute x2, starting transfers between devices, swap(): two = lax.ppermute(jnp.where(even, head, tail), axis, far)  13.4 us
    pallas_call x1, Pallas kernels, body(): pl.pallas_call(window, in_specs=[pl.BlockSpec(memory_space=pltpu.SMEM)] +...  12.1 us
    ppermute x2, waiting for transfers between devices, swap(): one = lax.ppermute(jnp.where(even, tail, head), axis, near)  5.6 us
  transfers between devices with their start and end apart: 4, of which 2 were waited for; matrix products, arithmetic and copies ran while one was open for 0% of the time, Pallas kernels for 0%

profile of v5, /device:TPU:1, one launch (start us, length us, event | category | flops | bytes accessed | tf_op | source)
XLA Modules:
  0.0 83.7 jit_solution(3174244363455817395)
XLA Ops:
  0.6 0.0 copy-start
  0.6 0.8 convert_bitcast_fusion
  1.4 0.1 copy-done
  1.5 0.1 slice_select_fusion.2
  1.6 7.8 %collective-permute-start.1 = (f32[5,16,192]{2,1,0:T(8,128)S(1)}, f32[5,16,192]{2,1,0:T(8,128)S(1)}, u32[]{:S(2)}, u32[]{:S(2)}) collective-permute-start(f32[5,16,192]{2,1,0:T(8,128)S(1)} %get-tuple-element.13), channel_id=1, source_target_pairs={{0,7},{1,2},{2,1},{3,4},{4,3},{5,6},{6,5},{7,0},{8,15},{9,10},{10,... | collective-permute-start | bytes 184328 | tf_op jit(solution)/shard_map/ppermute | solution.py:322
  9.5 1.9 %collective-permute-start = (f32[5,16,192]{2,1,0:T(8,128)S(1)}, f32[5,16,192]{2,1,0:T(8,128)S(1)}, u32[]{:S(2)}, u32[]{:S(2)}) collective-permute-start(f32[5,16,192]{2,1,0:T(8,128)S(1)} %get-tuple-element.14), channel_id=1, source_target_pairs={{0,1},{1,0},{2,3},{3,2},{4,5},{5,4},{6,7},{7,6},{8,9},{9,8},{10,11... | collective-permute-start | bytes 184328 | tf_op jit(solution)/shard_map/ppermute | solution.py:323
  11.4 0.0 collective-permute-done.1.side_two
  11.4 4.7 %collective-permute-done.side_one = f32[5,16,192]{2,1,0:T(8,128)S(1)} collective-permute-done((f32[5,16,192]{2,1,0:T(8,128)S(1)}, f32[5,16,192]{2,1,0:T(8,128)S(1)}, u32[]{:S(2)}, u32[]{:S(2)}) %collective-permute-start) | collective-permute-done | bytes 61472 | tf_op jit(solution)/shard_map/ppermute | solution.py:323
  16.2 0.1 pad_maximum_fusion
  16.3 5.5 %collective-permute-start.3 = (f32[5,8,768]{2,1,0:T(8,128)S(1)}, f32[5,8,768]{2,1,0:T(8,128)S(1)}, u32[]{:S(2)}, u32[]{:S(2)}) collective-permute-start(f32[5,8,768]{2,1,0:T(8,128)S(1)} %get-tuple-element.9), channel_id=1, source_target_pairs={{0,1016},{8,16},{16,8},{24,32},{32,24},{40,48},{48,40},{56,64},{64... | collective-permute-start | bytes 368648 | tf_op jit(solution)/shard_map/ppermute | solution.py:322
  21.9 15.3 %collective-permute-start.2 = (f32[5,8,768]{2,1,0:T(8,128)S(1)}, f32[5,8,768]{2,1,0:T(8,128)S(1)}, u32[]{:S(2)}, u32[]{:S(2)}) collective-permute-start(f32[5,8,768]{2,1,0:T(8,128)S(1)} %get-tuple-element.10), channel_id=1, source_target_pairs={{0,8},{8,0},{16,24},{24,16},{32,40},{40,32},{48,56},{56,48},{64,72... | collective-permute-start | bytes 368648 | tf_op jit(solution)/shard_map/ppermute | solution.py:323
  37.2 0.1 pad_maximum_fusion.2.zbase
  37.3 0.0 collective-permute-done.3.end_two
  37.3 0.9 %collective-permute-done.2.end_one = f32[5,8,768]{2,1,0:T(8,128)S(1)} collective-permute-done((f32[5,8,768]{2,1,0:T(8,128)S(1)}, f32[5,8,768]{2,1,0:T(8,128)S(1)}, u32[]{:S(2)}, u32[]{:S(2)}) %collective-permute-start.2) | collective-permute-done | bytes 122912 | tf_op jit(solution)/shard_map/ppermute | solution.py:323
  38.1 12.1 %lattice_window.1 = (f32[16,384]{1,0:T(8,128)}, f32[3,16,384]{2,1,0:T(8,128)}, f32[32,128]{1,0:T(8,128)S(1)}) custom-call(f32[4]{0:T(128)S(1)} %pad_maximum_fusion.2.zbase, f32[5,16,192]{2,1,0:T(8,128)S(1)} %collective-permute-done.side_one, f32[5,16,384]{2,1,0:T(8,128)S(1)} %pad_maximum_fusion.1.own, f32[5,16,192]{2,1,0:T(8,128)S(1)} %collective-permute-done.1.side_two, ...), custom_call_target="tpu_custom_call" | custom-call | tf_op jit(solution)/shard_map/lattice_window/pallas_call | solution.py:356
  50.3 8.8 %all_to_all.15 = f32[32,1,128]{2,1,0:T(1,128)S(1)} all-to-all(f32[32,1,128]{2,1,0:T(1,128)S(1)} %bitcast.13), channel_id=1, replica_groups={{13,14,15,512,513,514,515,516,517,518,519,520,521,522,523,524,525,526,5..., dimensions={0} | all-to-all | bytes 32768 | tf_op jit(solution)/shard_map/all_to_all | solution.py:314
  59.1 0.1 reduce_sum.18
  59.1 23.4 %all_to_all.16 = f32[32,1,128]{2,1,0:T(1,128)S(1)} all-to-all(f32[32,1,128]{2,1,0:T(1,128)S(1)} %broadcast_in_dim.11), channel_id=1, replica_groups={{288,304,320,336,352,368,384,400,416,432,448,464,480,496,0,16,32,48,64,..., dimensions={0} | all-to-all | bytes 32768 | tf_op jit(solution)/shard_map/all_to_all | solution.py:314
  (5 shorter events, 0.1 us)
Async XLA Ops:
  0.6 0.9 %copy-start = (f32[3,16,384]{2,1,0:T(8,128)S(1)}, f32[3,16,384]{2,1,0:T(8,128)}, u32[]{:S(2)}) copy-start(f32[3,16,384]{2,1,0:T(8,128)} %param.5) | copy-start | bytes 221188
  1.6 9.8 %collective-permute-start.1 = (f32[5,16,192]{2,1,0:T(8,128)S(1)}, f32[5,16,192]{2,1,0:T(8,128)S(1)}, u32[]{:S(2)}, u32[]{:S(2)}) collective-permute-start(f32[5,16,192]{2,1,0:T(8,128)S(1)} %get-tuple-element.13), channel_id=1, source_target_pairs={{0,7},{1,2},{2,1},{3,4},{4,3},{5,6},{6,5},{7,0},{8,15},{9,10},{10,... | collective-permute-start | bytes 184328 | tf_op jit(solution)/shard_map/ppermute | solution.py:322
  9.5 6.7 %collective-permute-start = (f32[5,16,192]{2,1,0:T(8,128)S(1)}, f32[5,16,192]{2,1,0:T(8,128)S(1)}, u32[]{:S(2)}, u32[]{:S(2)}) collective-permute-start(f32[5,16,192]{2,1,0:T(8,128)S(1)} %get-tuple-element.14), channel_id=1, source_target_pairs={{0,1},{1,0},{2,3},{3,2},{4,5},{5,4},{6,7},{7,6},{8,9},{9,8},{10,11... | collective-permute-start | bytes 184328 | tf_op jit(solution)/shard_map/ppermute | solution.py:323
  16.3 20.9 %collective-permute-start.3 = (f32[5,8,768]{2,1,0:T(8,128)S(1)}, f32[5,8,768]{2,1,0:T(8,128)S(1)}, u32[]{:S(2)}, u32[]{:S(2)}) collective-permute-start(f32[5,8,768]{2,1,0:T(8,128)S(1)} %get-tuple-element.9), channel_id=1, source_target_pairs={{0,1016},{8,16},{16,8},{24,32},{32,24},{40,48},{48,40},{56,64},{64... | collective-permute-start | bytes 368648 | tf_op jit(solution)/shard_map/ppermute | solution.py:322
  21.9 16.2 %collective-permute-start.2 = (f32[5,8,768]{2,1,0:T(8,128)S(1)}, f32[5,8,768]{2,1,0:T(8,128)S(1)}, u32[]{:S(2)}, u32[]{:S(2)}) collective-permute-start(f32[5,8,768]{2,1,0:T(8,128)S(1)} %get-tuple-element.10), channel_id=1, source_target_pairs={{0,8},{8,0},{16,24},{24,16},{32,40},{40,32},{48,56},{56,48},{64,72... | collective-permute-start | bytes 368648 | tf_op jit(solution)/shard_map/ppermute | solution.py:323

commit v6 on v5

--- a/solution.py
+++ b/solution.py
@@ -317,8 +317,7 @@
 
 def swap(axis, count, even, head, tail):
     near = [(i, i ^ 1) for i in range(count)]
-    far = [(i, (((i + 1) % count) ^ 1) - 1) for i in range(count)]
-    far = [(i, j % count) for i, j in far]
+    far = [(i, ((i + 1) ^ 1) - 1) for i in range(1, count - 1)]
     two = lax.ppermute(jnp.where(even, head, tail), axis, far)
     one = lax.ppermute(jnp.where(even, tail, head), axis, near)
     return one, two

time: 84.6 us -> 83.4 us (0.986)
  blocking collectives: 32.2 us -> 41.1 us
  starting transfers between devices: 30.6 us -> 23.4 us
  waiting for transfers between devices: 5.6 us -> 2.65 us
    all_to_all x2, blocking collectives: 32.2 us -> 41.1 us  [all_sum(): lax.all_to_all(part, axes, 0, 0, tiled=True, axis_index_groups=order)]
    ppermute x2, starting transfers between devices: 13.4 us -> 5.92 us  [swap(): two = lax.ppermute(jnp.where(even, head, tail), axis, far)]
    ppermute x2, waiting for transfers between devices: 5.6 us -> 2.65 us  [swap(): one = lax.ppermute(jnp.where(even, tail, head), axis, near)]
where the time goes in v6:
time: 83.4 us; the launch traced here: 82.5 us
  blocking collectives  41.1 us (49%)
  starting transfers between devices  23.4 us (28%)
  Pallas kernels  12.1 us (15%)
  waiting for transfers between devices  2.65 us (3%)
  between operations  1.92 us (2%)
  other arithmetic  1.2 us (1%)
    all_to_all x2, blocking collectives, all_sum(): lax.all_to_all(part, axes, 0, 0, tiled=True, axis_index_groups=order)  41.1 us
    ppermute x2, starting transfers between devices, swap(): one = lax.ppermute(jnp.where(even, tail, head), axis, near)  17.5 us
    pallas_call x1, Pallas kernels, body(): pl.pallas_call(window, in_specs=[pl.BlockSpec(memory_space=pltpu.SMEM)] +...  12.1 us
    ppermute x2, starting transfers between devices, swap(): two = lax.ppermute(jnp.where(even, head, tail), axis, far)  5.92 us
    ppermute x2, waiting for transfers between devices, swap(): one = lax.ppermute(jnp.where(even, tail, head), axis, near)  2.65 us
  transfers between devices with their start and end apart: 4, of which 2 were waited for; matrix products, arithmetic and copies ran while one was open for 0% of the time, Pallas kernels for 0%

profile of v6, /device:TPU:1, one launch (start us, length us, event | category | flops | bytes accessed | tf_op | source)
XLA Modules:
  0.0 82.5 jit_solution(13291378541616864354)
XLA Ops:
  0.6 0.0 copy-start
  0.6 0.8 convert_bitcast_fusion
  1.4 0.1 copy-done
  1.5 0.1 slice_select_fusion.2
  1.6 0.7 collective-permute-start.1
  2.3 7.9 %collective-permute-start = (f32[5,16,192]{2,1,0:T(8,128)S(1)}, f32[5,16,192]{2,1,0:T(8,128)S(1)}, u32[]{:S(2)}, u32[]{:S(2)}) collective-permute-start(f32[5,16,192]{2,1,0:T(8,128)S(1)} %get-tuple-element.14), channel_id=1, source_target_pairs={{0,1},{1,0},{2,3},{3,2},{4,5},{5,4},{6,7},{7,6},{8,9},{9,8},{10,11... | collective-permute-start | bytes 184328 | tf_op jit(solution)/shard_map/ppermute | solution.py:322
  10.2 0.0 collective-permute-done.1.side_two
  10.2 1.8 %collective-permute-done.side_one = f32[5,16,192]{2,1,0:T(8,128)S(1)} collective-permute-done((f32[5,16,192]{2,1,0:T(8,128)S(1)}, f32[5,16,192]{2,1,0:T(8,128)S(1)}, u32[]{:S(2)}, u32[]{:S(2)}) %collective-permute-start) | collective-permute-done | bytes 61472 | tf_op jit(solution)/shard_map/ppermute | solution.py:322
  12.0 0.1 pad_maximum_fusion
  12.2 5.3 %collective-permute-start.3 = (f32[5,8,768]{2,1,0:T(8,128)S(1)}, f32[5,8,768]{2,1,0:T(8,128)S(1)}, u32[]{:S(2)}, u32[]{:S(2)}) collective-permute-start(f32[5,8,768]{2,1,0:T(8,128)S(1)} %get-tuple-element.9), channel_id=1, source_target_pairs={{8,16},{16,8},{24,32},{32,24},{40,48},{48,40},{56,64},{64,56},{72,... | collective-permute-start | bytes 368648 | tf_op jit(solution)/shard_map/ppermute | solution.py:321
  17.4 9.6 %collective-permute-start.2 = (f32[5,8,768]{2,1,0:T(8,128)S(1)}, f32[5,8,768]{2,1,0:T(8,128)S(1)}, u32[]{:S(2)}, u32[]{:S(2)}) collective-permute-start(f32[5,8,768]{2,1,0:T(8,128)S(1)} %get-tuple-element.10), channel_id=1, source_target_pairs={{0,8},{8,0},{16,24},{24,16},{32,40},{40,32},{48,56},{56,48},{64,72... | collective-permute-start | bytes 368648 | tf_op jit(solution)/shard_map/ppermute | solution.py:322
  27.1 0.1 pad_maximum_fusion.2.zbase
  27.2 0.0 collective-permute-done.3.end_two
  27.2 0.9 %collective-permute-done.2.end_one = f32[5,8,768]{2,1,0:T(8,128)S(1)} collective-permute-done((f32[5,8,768]{2,1,0:T(8,128)S(1)}, f32[5,8,768]{2,1,0:T(8,128)S(1)}, u32[]{:S(2)}, u32[]{:S(2)}) %collective-permute-start.2) | collective-permute-done | bytes 122912 | tf_op jit(solution)/shard_map/ppermute | solution.py:322
  28.0 12.1 %lattice_window.1 = (f32[16,384]{1,0:T(8,128)}, f32[3,16,384]{2,1,0:T(8,128)}, f32[32,128]{1,0:T(8,128)S(1)}) custom-call(f32[4]{0:T(128)S(1)} %pad_maximum_fusion.2.zbase, f32[5,16,192]{2,1,0:T(8,128)S(1)} %collective-permute-done.side_one, f32[5,16,384]{2,1,0:T(8,128)S(1)} %pad_maximum_fusion.1.own, f32[5,16,192]{2,1,0:T(8,128)S(1)} %collective-permute-done.1.side_two, ...), custom_call_target="tpu_custom_call" | custom-call | tf_op jit(solution)/shard_map/lattice_window/pallas_call | solution.py:355
  40.2 17.6 %all_to_all.15 = f32[32,1,128]{2,1,0:T(1,128)S(1)} all-to-all(f32[32,1,128]{2,1,0:T(1,128)S(1)} %bitcast.13), channel_id=1, replica_groups={{13,14,15,512,513,514,515,516,517,518,519,520,521,522,523,524,525,526,5..., dimensions={0} | all-to-all | bytes 32768 | tf_op jit(solution)/shard_map/all_to_all | solution.py:314
  57.7 0.1 reduce_sum.18
  57.8 23.5 %all_to_all.16 = f32[32,1,128]{2,1,0:T(1,128)S(1)} all-to-all(f32[32,1,128]{2,1,0:T(1,128)S(1)} %broadcast_in_dim.11), channel_id=1, replica_groups={{288,304,320,336,352,368,384,400,416,432,448,464,480,496,0,16,32,48,64,..., dimensions={0} | all-to-all | bytes 32768 | tf_op jit(solution)/shard_map/all_to_all | solution.py:314
  (5 shorter events, 0.1 us)
Async XLA Ops:
  0.6 0.9 %copy-start = (f32[3,16,384]{2,1,0:T(8,128)S(1)}, f32[3,16,384]{2,1,0:T(8,128)}, u32[]{:S(2)}) copy-start(f32[3,16,384]{2,1,0:T(8,128)} %param.5) | copy-start | bytes 221188
  1.6 8.6 %collective-permute-start.1 = (f32[5,16,192]{2,1,0:T(8,128)S(1)}, f32[5,16,192]{2,1,0:T(8,128)S(1)}, u32[]{:S(2)}, u32[]{:S(2)}) collective-permute-start(f32[5,16,192]{2,1,0:T(8,128)S(1)} %get-tuple-element.13), channel_id=1, source_target_pairs={{1,2},{2,1},{3,4},{4,3},{5,6},{6,5},{9,10},{10,9},{11,12},{12,11},... | collective-permute-start | bytes 184328 | tf_op jit(solution)/shard_map/ppermute | solution.py:321
  2.3 9.7 %collective-permute-start = (f32[5,16,192]{2,1,0:T(8,128)S(1)}, f32[5,16,192]{2,1,0:T(8,128)S(1)}, u32[]{:S(2)}, u32[]{:S(2)}) collective-permute-start(f32[5,16,192]{2,1,0:T(8,128)S(1)} %get-tuple-element.14), channel_id=1, source_target_pairs={{0,1},{1,0},{2,3},{3,2},{4,5},{5,4},{6,7},{7,6},{8,9},{9,8},{10,11... | collective-permute-start | bytes 184328 | tf_op jit(solution)/shard_map/ppermute | solution.py:322
  12.2 15.0 %collective-permute-start.3 = (f32[5,8,768]{2,1,0:T(8,128)S(1)}, f32[5,8,768]{2,1,0:T(8,128)S(1)}, u32[]{:S(2)}, u32[]{:S(2)}) collective-permute-start(f32[5,8,768]{2,1,0:T(8,128)S(1)} %get-tuple-element.9), channel_id=1, source_target_pairs={{8,16},{16,8},{24,32},{32,24},{40,48},{48,40},{56,64},{64,56},{72,... | collective-permute-start | bytes 368648 | tf_op jit(solution)/shard_map/ppermute | solution.py:321
  17.4 10.6 %collective-permute-start.2 = (f32[5,8,768]{2,1,0:T(8,128)S(1)}, f32[5,8,768]{2,1,0:T(8,128)S(1)}, u32[]{:S(2)}, u32[]{:S(2)}) collective-permute-start(f32[5,8,768]{2,1,0:T(8,128)S(1)} %get-tuple-element.10), channel_id=1, source_target_pairs={{0,8},{8,0},{16,24},{24,16},{32,40},{40,32},{48,56},{56,48},{64,72... | collective-permute-start | bytes 368648 | tf_op jit(solution)/shard_map/ppermute | solution.py:322

commit v7 on v6

--- a/solution.py
+++ b/solution.py
@@ -195,23 +195,16 @@
     return f, g
 
 
-def window(zbase, side_one, own, side_two, end_one, end_two, temp_out, flow_out, part_out,
+def window(zbase, side_one, tall, side_two, temp_out, flow_out, part_out,
            stage, inp, pops, wa, wb, res):
     height = zbase[1]
-    even_y, even_z = zbase[2] > 0.5, zbase[3] > 0.5
-
-    def low_high(even, one, two):
-        return jnp.where(even, two, one), jnp.where(even, one, two)
-
+    even_y = zbase[2] > 0.5
     for a in range(5):
-        left, right = low_high(even_y, side_one[a], side_two[a])
-        top, bot = low_high(even_z, end_one[a], end_two[a])
-        blocks = (left, own[a, :, 0:192], own[a, :, 192:384], right)
+        left = jnp.where(even_y, side_two[a], side_one[a])
+        right = jnp.where(even_y, side_one[a], side_two[a])
+        blocks = (left, tall[a, :, 0:192], tall[a, :, 192:384], right)
         for q in range(4):
-            r0 = 32 * q
-            stage[a, r0 : r0 + 8, 0:192] = top[:, 192 * q : 192 * q + 192]
-            stage[a, r0 + 8 : r0 + 24, 0:192] = blocks[q]
-            stage[a, r0 + 24 : r0 + 32, 0:192] = bot[:, 192 * q : 192 * q + 192]
+            stage[a, 32 * q : 32 * q + 32, 0:192] = blocks[q]
         inp[a, 0:16] = stage[a, :, 0:128].T.reshape(16, 8, 128)
         inp[a, 16:24] = stage[a, :, 128:256].T[0:64].reshape(8, 8, 128)
 
@@ -337,24 +330,23 @@
         rim = HALO * NX
         even_y = (lax.axis_index(gy) & 1) == 0
         even_z = (lax.axis_index(gz[-1]) & 1) == 0
-        sides = swap(gy, n_gy, even_y, own[:, :, :rim], own[:, :, cells - rim :])
-        left = jnp.where(even_y, sides[1], sides[0])
-        right = jnp.where(even_y, sides[0], sides[1])
-        wide = jnp.concatenate([left, own, right], axis=2)
-        ends = swap(gz, n_gz, even_z, wide[:, :HALO], wide[:, slab - HALO :])
+        ends = swap(gz, n_gz, even_z, own[:, :HALO], own[:, slab - HALO :])
+        top = jnp.where(even_z, ends[1], ends[0])
+        bot = jnp.where(even_z, ends[0], ends[1])
+        tall = jnp.concatenate([top, own, bot], axis=1)
+        sides = swap(gy, n_gy, even_y, tall[:, :, :rim], tall[:, :, cells - rim :])
         zbase = jnp.stack(
             [
                 (lax.axis_index(gz) * slab - HALO).astype(jnp.float32),
                 jnp.float32(height),
                 even_y.astype(jnp.float32),
-                even_z.astype(jnp.float32),
             ]
         )
         vmem = pl.BlockSpec(memory_space=pltpu.VMEM)
         f32 = jnp.float32
         temp, flow, part = pl.pallas_call(
             window,
-            in_specs=[pl.BlockSpec(memory_space=pltpu.SMEM)] + [vmem] * 5,
+            in_specs=[pl.BlockSpec(memory_space=pltpu.SMEM)] + [vmem] * 3,
             out_specs=[vmem] * 3,
             out_shape=[
                 jax.ShapeDtypeStruct((slab, cells), f32),
@@ -364,7 +356,7 @@
             scratch_shapes=SCRATCH,
             compiler_params=pltpu.CompilerParams(vmem_limit_bytes=40 * 1024 * 1024),
             name="lattice_window",
-        )(zbase, sides[0], own, sides[1], ends[0], ends[1])
+        )(zbase, sides[0], tall, sides[1])
         line = all_sum(part, near, n_near, n_gy + 5 * n_gy // 8)
         line = all_sum(jnp.broadcast_to(line, (n_far, 128)), far, n_far, 9 * n_far // 16)
         return temp, flow, line[0] * (2.0 / (NX * height))

time: 83.4 us -> 85.4 us (1.024)
  waiting for transfers between devices: 2.65 us -> 7.67 us
  starting transfers between devices: 23.4 us -> 19.3 us
  blocking collectives: 41.1 us -> 42.3 us
    ppermute x2, waiting for transfers between devices: 2.65 us -> 7.67 us  [swap(): one = lax.ppermute(jnp.where(even, tail, head), axis, near)]
    ppermute x2, starting transfers between devices: 17.5 us -> 13.7 us  [swap(): one = lax.ppermute(jnp.where(even, tail, head), axis, near)]
    all_to_all x2, blocking collectives: 41.1 us -> 42.3 us  [all_sum(): lax.all_to_all(part, axes, 0, 0, tiled=True, axis_index_groups=order)]
where the time goes in v7:
time: 85.4 us; the launch traced here: 84.5 us
  blocking collectives  42.3 us (50%)
  starting transfers between devices  19.3 us (23%)
  Pallas kernels  12.1 us (14%)
  waiting for transfers between devices  7.67 us (9%)
  between operations  1.91 us (2%)
  other arithmetic  1.1 us (1%)
    all_to_all x2, blocking collectives, all_sum(): lax.all_to_all(part, axes, 0, 0, tiled=True, axis_index_groups=order)  42.3 us
    ppermute x2, starting transfers between devices, swap(): one = lax.ppermute(jnp.where(even, tail, head), axis, near)  13.7 us
    pallas_call x1, Pallas kernels, body(): pl.pallas_call(window, in_specs=[pl.BlockSpec(memory_space=pltpu.SMEM)] +...  12.1 us
    ppermute x2, waiting for transfers between devices, swap(): one = lax.ppermute(jnp.where(even, tail, head), axis, near)  7.67 us
    ppermute x2, starting transfers between devices, swap(): two = lax.ppermute(jnp.where(even, head, tail), axis, far)  5.61 us
  transfers between devices with their start and end apart: 4, of which 2 were waited for; matrix products, arithmetic and copies ran while one was open for 0% of the time, Pallas kernels for 0%

profile of v7, /device:TPU:1, one launch (start us, length us, event | category | flops | bytes accessed | tf_op | source)
XLA Modules:
  0.0 84.5 jit_solution(17286733057241534983)
XLA Ops:
  0.6 0.0 copy-start
  0.6 0.8 convert_bitcast_fusion
  1.4 0.1 copy-done
  1.5 4.9 %collective-permute-start = (f32[5,8,384]{2,1,0:T(8,128)S(1)}, f32[5,8,384]{2,1,0:T(8,128)S(1)}, u32[]{:S(2)}, u32[]{:S(2)}) collective-permute-start(f32[5,8,384]{2,1,0:T(8,128)S(1)} %get-tuple-element.13), channel_id=1, source_target_pairs={{8,16},{16,8},{24,32},{32,24},{40,48},{48,40},{56,64},{64,56},{72,... | collective-permute-start | bytes 184328 | tf_op jit(solution)/shard_map/ppermute | solution.py:314
  6.5 11.8 %collective-permute-start.1 = (f32[5,8,384]{2,1,0:T(8,128)S(1)}, f32[5,8,384]{2,1,0:T(8,128)S(1)}, u32[]{:S(2)}, u32[]{:S(2)}) collective-permute-start(f32[5,8,384]{2,1,0:T(8,128)S(1)} %get-tuple-element.14), channel_id=1, source_target_pairs={{0,8},{8,0},{16,24},{24,16},{32,40},{40,32},{48,56},{56,48},{64,72... | collective-permute-start | bytes 184328 | tf_op jit(solution)/shard_map/ppermute | solution.py:315
  18.3 0.0 collective-permute-done
  18.3 0.9 %collective-permute-done.1 = f32[5,8,384]{2,1,0:T(8,128)S(1)} collective-permute-done((f32[5,8,384]{2,1,0:T(8,128)S(1)}, f32[5,8,384]{2,1,0:T(8,128)S(1)}, u32[]{:S(2)}, u32[]{:S(2)}) %collective-permute-start.1) | collective-permute-done | bytes 61472 | tf_op jit(solution)/shard_map/ppermute | solution.py:315
  19.2 0.1 slice_select_fusion
  19.3 0.7 collective-permute-start.3
  20.0 1.9 %collective-permute-start.2 = (f32[5,32,192]{2,1,0:T(8,128)S(1)}, f32[5,32,192]{2,1,0:T(8,128)S(1)}, u32[]{:S(2)}, u32[]{:S(2)}) collective-permute-start(f32[5,32,192]{2,1,0:T(8,128)S(1)} %get-tuple-element.10), channel_id=1, source_target_pairs={{0,1},{1,0},{2,3},{3,2},{4,5},{5,4},{6,7},{7,6},{8,9},{9,8},{10,11... | collective-permute-start | bytes 368648 | tf_op jit(solution)/shard_map/ppermute | solution.py:315
  21.9 0.1 pad_maximum_fusion.2.zbase
  22.0 0.0 collective-permute-done.3.side_two
  22.0 6.8 %collective-permute-done.2.side_one = f32[5,32,192]{2,1,0:T(8,128)S(1)} collective-permute-done((f32[5,32,192]{2,1,0:T(8,128)S(1)}, f32[5,32,192]{2,1,0:T(8,128)S(1)}, u32[]{:S(2)}, u32[]{:S(2)}) %collective-permute-start.2) | collective-permute-done | bytes 122912 | tf_op jit(solution)/shard_map/ppermute | solution.py:315
  28.8 12.1 %lattice_window.1 = (f32[16,384]{1,0:T(8,128)}, f32[3,16,384]{2,1,0:T(8,128)}, f32[32,128]{1,0:T(8,128)S(1)}) custom-call(f32[3]{0:T(128)S(1)} %pad_maximum_fusion.2.zbase, f32[5,32,192]{2,1,0:T(8,128)S(1)} %collective-permute-done.2.side_one, f32[5,32,384]{2,1,0:T(8,128)S(1)} %pad_maximum_fusion.tall, f32[5,32,192]{2,1,0:T(8,128)S(1)} %collective-permute-done.3.side_two), custom_call_target="tpu_custom_call" | custom-call | tf_op jit(solution)/shard_map/lattice_window/pallas_call | solution.py:347
  40.9 19.3 %all_to_all.15 = f32[32,1,128]{2,1,0:T(1,128)S(1)} all-to-all(f32[32,1,128]{2,1,0:T(1,128)S(1)} %bitcast.12), channel_id=1, replica_groups={{13,14,15,512,513,514,515,516,517,518,519,520,521,522,523,524,525,526,5..., dimensions={0} | all-to-all | bytes 32768 | tf_op jit(solution)/shard_map/all_to_all | solution.py:307
  60.3 0.1 reduce_sum.18
  60.3 23.0 %all_to_all.16 = f32[32,1,128]{2,1,0:T(1,128)S(1)} all-to-all(f32[32,1,128]{2,1,0:T(1,128)S(1)} %broadcast_in_dim.11), channel_id=1, replica_groups={{288,304,320,336,352,368,384,400,416,432,448,464,480,496,0,16,32,48,64,..., dimensions={0} | all-to-all | bytes 32768 | tf_op jit(solution)/shard_map/all_to_all | solution.py:307
  (6 shorter events, 0.1 us)
Async XLA Ops:
  0.6 0.9 %copy-start = (f32[3,16,384]{2,1,0:T(8,128)S(1)}, f32[3,16,384]{2,1,0:T(8,128)}, u32[]{:S(2)}) copy-start(f32[3,16,384]{2,1,0:T(8,128)} %param.5) | copy-start | bytes 221188
  1.5 16.8 %collective-permute-start = (f32[5,8,384]{2,1,0:T(8,128)S(1)}, f32[5,8,384]{2,1,0:T(8,128)S(1)}, u32[]{:S(2)}, u32[]{:S(2)}) collective-permute-start(f32[5,8,384]{2,1,0:T(8,128)S(1)} %get-tuple-element.13), channel_id=1, source_target_pairs={{8,16},{16,8},{24,32},{32,24},{40,48},{48,40},{56,64},{64,56},{72,... | collective-permute-start | bytes 184328 | tf_op jit(solution)/shard_map/ppermute | solution.py:314
  6.5 12.7 %collective-permute-start.1 = (f32[5,8,384]{2,1,0:T(8,128)S(1)}, f32[5,8,384]{2,1,0:T(8,128)S(1)}, u32[]{:S(2)}, u32[]{:S(2)}) collective-permute-start(f32[5,8,384]{2,1,0:T(8,128)S(1)} %get-tuple-element.14), channel_id=1, source_target_pairs={{0,8},{8,0},{16,24},{24,16},{32,40},{40,32},{48,56},{56,48},{64,72... | collective-permute-start | bytes 184328 | tf_op jit(solution)/shard_map/ppermute | solution.py:315
  19.3 2.7 %collective-permute-start.3 = (f32[5,32,192]{2,1,0:T(8,128)S(1)}, f32[5,32,192]{2,1,0:T(8,128)S(1)}, u32[]{:S(2)}, u32[]{:S(2)}) collective-permute-start(f32[5,32,192]{2,1,0:T(8,128)S(1)} %get-tuple-element.9), channel_id=1, source_target_pairs={{1,2},{2,1},{3,4},{4,3},{5,6},{6,5},{9,10},{10,9},{11,12},{12,11},... | collective-permute-start | bytes 368648 | tf_op jit(solution)/shard_map/ppermute | solution.py:314
  20.0 8.8 %collective-permute-start.2 = (f32[5,32,192]{2,1,0:T(8,128)S(1)}, f32[5,32,192]{2,1,0:T(8,128)S(1)}, u32[]{:S(2)}, u32[]{:S(2)}) collective-permute-start(f32[5,32,192]{2,1,0:T(8,128)S(1)} %get-tuple-element.10), channel_id=1, source_target_pairs={{0,1},{1,0},{2,3},{3,2},{4,5},{5,4},{6,7},{7,6},{8,9},{9,8},{10,11... | collective-permute-start | bytes 368648 | tf_op jit(solution)/shard_map/ppermute | solution.py:315

commit v8 on v6

--- a/solution.py
+++ b/solution.py
@@ -260,11 +260,11 @@
                 put_all(dst, s, xt, collide(f, g))
             return c
 
-        lax.fori_loop(0, NS, line, 0, unroll=4)
+        lax.fori_loop(0, NS, line, 0, unroll=True)
         copies(dst)
         return carry
 
-    lax.fori_loop(1, STEPS, step, 0)
+    lax.fori_loop(1, STEPS, step, 0, unroll=True)
     src = pops.at[(STEPS - 1) % 2]
 
     def last(s, total):

time: 83.4 us -> 79.6 us (0.954)
  Pallas kernels: 12.1 us -> 8.39 us
    pallas_call x1, Pallas kernels: 12.1 us -> 8.39 us  [body(): pl.pallas_call(window, in_specs=[pl.BlockSpec(memory_space=pltpu.SMEM)] +...]
where the time goes in v8:
time: 79.6 us; the launch traced here: 78.7 us
  blocking collectives  41.1 us (52%)
  starting transfers between devices  23.4 us (29%)
  Pallas kernels  8.39 us (11%)
  waiting for transfers between devices  2.65 us (3%)
  between operations  1.92 us (2%)
  other arithmetic  1.2 us (2%)
    all_to_all x2, blocking collectives, all_sum(): lax.all_to_all(part, axes, 0, 0, tiled=True, axis_index_groups=order)  41.1 us
    ppermute x2, starting transfers between devices, swap(): one = lax.ppermute(jnp.where(even, tail, head), axis, near)  17.5 us
    pallas_call x1, Pallas kernels, body(): pl.pallas_call(window, in_specs=[pl.BlockSpec(memory_space=pltpu.SMEM)] +...  8.39 us
    ppermute x2, starting transfers between devices, swap(): two = lax.ppermute(jnp.where(even, head, tail), axis, far)  5.92 us
    ppermute x2, waiting for transfers between devices, swap(): one = lax.ppermute(jnp.where(even, tail, head), axis, near)  2.65 us
  transfers between devices with their start and end apart: 4, of which 2 were waited for; matrix products, arithmetic and copies ran while one was open for 0% of the time, Pallas kernels for 0%

profile of v8, /device:TPU:1, one launch (start us, length us, event | category | flops | bytes accessed | tf_op | source)
XLA Modules:
  0.0 78.7 jit_solution(2334572508679603159)
XLA Ops:
  0.6 0.0 copy-start
  0.6 0.8 %convert_bitcast_fusion = (f32[1,16,384]{2,1,0:T(8,128)S(1)}, f32[1,16,384]{2,1,0:T(8,128)S(1)}) fusion(s32[16,384]{1,0:T(8,128)} %param.4, s32[16,384]{1,0:T(8,128)} %param.3), kind=kLoop, calls=%fused_computation.8 | loop fusion | flops 12288 | bytes 98304 | tf_op jit(solution)/shard_map/broadcast_in_dim | solution.py:333
  1.4 0.1 copy-done
  1.5 0.1 slice_select_fusion.2
  1.6 0.7 collective-permute-start.1
  2.3 7.9 %collective-permute-start = (f32[5,16,192]{2,1,0:T(8,128)S(1)}, f32[5,16,192]{2,1,0:T(8,128)S(1)}, u32[]{:S(2)}, u32[]{:S(2)}) collective-permute-start(f32[5,16,192]{2,1,0:T(8,128)S(1)} %get-tuple-element.14), channel_id=1, source_target_pairs={{0,1},{1,0},{2,3},{3,2},{4,5},{5,4},{6,7},{7,6},{8,9},{9,8},{10,11... | collective-permute-start | bytes 184328 | tf_op jit(solution)/shard_map/ppermute | solution.py:322
  10.2 0.0 collective-permute-done.1.side_two
  10.2 1.8 %collective-permute-done.side_one = f32[5,16,192]{2,1,0:T(8,128)S(1)} collective-permute-done((f32[5,16,192]{2,1,0:T(8,128)S(1)}, f32[5,16,192]{2,1,0:T(8,128)S(1)}, u32[]{:S(2)}, u32[]{:S(2)}) %collective-permute-start) | collective-permute-done | bytes 61472 | tf_op jit(solution)/shard_map/ppermute | solution.py:322
  12.0 0.1 pad_maximum_fusion
  12.2 5.3 %collective-permute-start.3 = (f32[5,8,768]{2,1,0:T(8,128)S(1)}, f32[5,8,768]{2,1,0:T(8,128)S(1)}, u32[]{:S(2)}, u32[]{:S(2)}) collective-permute-start(f32[5,8,768]{2,1,0:T(8,128)S(1)} %get-tuple-element.9), channel_id=1, source_target_pairs={{8,16},{16,8},{24,32},{32,24},{40,48},{48,40},{56,64},{64,56},{72,... | collective-permute-start | bytes 368648 | tf_op jit(solution)/shard_map/ppermute | solution.py:321
  17.4 9.6 %collective-permute-start.2 = (f32[5,8,768]{2,1,0:T(8,128)S(1)}, f32[5,8,768]{2,1,0:T(8,128)S(1)}, u32[]{:S(2)}, u32[]{:S(2)}) collective-permute-start(f32[5,8,768]{2,1,0:T(8,128)S(1)} %get-tuple-element.10), channel_id=1, source_target_pairs={{0,8},{8,0},{16,24},{24,16},{32,40},{40,32},{48,56},{56,48},{64,72... | collective-permute-start | bytes 368648 | tf_op jit(solution)/shard_map/ppermute | solution.py:322
  27.1 0.1 pad_maximum_fusion.2.zbase
  27.2 0.0 collective-permute-done.3.end_two
  27.2 0.9 %collective-permute-done.2.end_one = f32[5,8,768]{2,1,0:T(8,128)S(1)} collective-permute-done((f32[5,8,768]{2,1,0:T(8,128)S(1)}, f32[5,8,768]{2,1,0:T(8,128)S(1)}, u32[]{:S(2)}, u32[]{:S(2)}) %collective-permute-start.2) | collective-permute-done | bytes 122912 | tf_op jit(solution)/shard_map/ppermute | solution.py:322
  28.0 8.4 %lattice_window.1 = (f32[16,384]{1,0:T(8,128)}, f32[3,16,384]{2,1,0:T(8,128)}, f32[32,128]{1,0:T(8,128)S(1)}) custom-call(f32[4]{0:T(128)S(1)} %pad_maximum_fusion.2.zbase, f32[5,16,192]{2,1,0:T(8,128)S(1)} %collective-permute-done.side_one, f32[5,16,384]{2,1,0:T(8,128)S(1)} %pad_maximum_fusion.1.own, f32[5,16,192]{2,1,0:T(8,128)S(1)} %collective-permute-done.1.side_two, ...), custom_call_target="tpu_custom_call" | custom-call | tf_op jit(solution)/shard_map/lattice_window/pallas_call | solution.py:355
  36.4 17.6 %all_to_all.15 = f32[32,1,128]{2,1,0:T(1,128)S(1)} all-to-all(f32[32,1,128]{2,1,0:T(1,128)S(1)} %bitcast.13), channel_id=1, replica_groups={{13,14,15,512,513,514,515,516,517,518,519,520,521,522,523,524,525,526,5..., dimensions={0} | all-to-all | bytes 32768 | tf_op jit(solution)/shard_map/all_to_all | solution.py:314
  54.0 0.1 reduce_sum.18
  54.0 23.5 %all_to_all.16 = f32[32,1,128]{2,1,0:T(1,128)S(1)} all-to-all(f32[32,1,128]{2,1,0:T(1,128)S(1)} %broadcast_in_dim.11), channel_id=1, replica_groups={{288,304,320,336,352,368,384,400,416,432,448,464,480,496,0,16,32,48,64,..., dimensions={0} | all-to-all | bytes 32768 | tf_op jit(solution)/shard_map/all_to_all | solution.py:314
  (5 shorter events, 0.1 us)
Async XLA Ops:
  0.6 0.9 %copy-start = (f32[3,16,384]{2,1,0:T(8,128)S(1)}, f32[3,16,384]{2,1,0:T(8,128)}, u32[]{:S(2)}) copy-start(f32[3,16,384]{2,1,0:T(8,128)} %param.5) | copy-start | bytes 221188
  1.6 8.6 %collective-permute-start.1 = (f32[5,16,192]{2,1,0:T(8,128)S(1)}, f32[5,16,192]{2,1,0:T(8,128)S(1)}, u32[]{:S(2)}, u32[]{:S(2)}) collective-permute-start(f32[5,16,192]{2,1,0:T(8,128)S(1)} %get-tuple-element.13), channel_id=1, source_target_pairs={{1,2},{2,1},{3,4},{4,3},{5,6},{6,5},{9,10},{10,9},{11,12},{12,11},... | collective-permute-start | bytes 184328 | tf_op jit(solution)/shard_map/ppermute | solution.py:321
  2.3 9.7 %collective-permute-start = (f32[5,16,192]{2,1,0:T(8,128)S(1)}, f32[5,16,192]{2,1,0:T(8,128)S(1)}, u32[]{:S(2)}, u32[]{:S(2)}) collective-permute-start(f32[5,16,192]{2,1,0:T(8,128)S(1)} %get-tuple-element.14), channel_id=1, source_target_pairs={{0,1},{1,0},{2,3},{3,2},{4,5},{5,4},{6,7},{7,6},{8,9},{9,8},{10,11... | collective-permute-start | bytes 184328 | tf_op jit(solution)/shard_map/ppermute | solution.py:322
  12.2 15.0 %collective-permute-start.3 = (f32[5,8,768]{2,1,0:T(8,128)S(1)}, f32[5,8,768]{2,1,0:T(8,128)S(1)}, u32[]{:S(2)}, u32[]{:S(2)}) collective-permute-start(f32[5,8,768]{2,1,0:T(8,128)S(1)} %get-tuple-element.9), channel_id=1, source_target_pairs={{8,16},{16,8},{24,32},{32,24},{40,48},{48,40},{56,64},{64,56},{72,... | collective-permute-start | bytes 368648 | tf_op jit(solution)/shard_map/ppermute | solution.py:321
  17.4 10.6 %collective-permute-start.2 = (f32[5,8,768]{2,1,0:T(8,128)S(1)}, f32[5,8,768]{2,1,0:T(8,128)S(1)}, u32[]{:S(2)}, u32[]{:S(2)}) collective-permute-start(f32[5,8,768]{2,1,0:T(8,128)S(1)} %get-tuple-element.10), channel_id=1, source_target_pairs={{0,8},{8,0},{16,24},{24,16},{32,40},{40,32},{48,56},{56,48},{64,72... | collective-permute-start | bytes 368648 | tf_op jit(solution)/shard_map/ppermute | solution.py:322
